TPU v7x, 32 devices: a whole 2x2x4 slice. The times are simulated.
32 devices in a mesh: dp: 16 (over z, y, x), blk: 2 (over core).
Axes of the slice: x: 2, y: 2, z: 4, core: 2. Of those that a mesh axis runs over, the one named last changes fastest.
Arguments:
- tokens: bfloat16 [32, 1252, 768], P('dp', 'blk'), may hold values from -6 to 6
- counts: int32 [32], P('dp'), may hold values from 10 to 104, as said below
- attend_gain: bfloat16 [768], P(('dp', 'blk')), may hold values from 0.099609375 to 1.8984375
- attend_shift: bfloat16 [768], P(('dp', 'blk')), may hold values from -2.5 to 2.5
- merged_weight: bfloat16 [768, 2304], P(('dp', 'blk')), may hold values from -0.21875 to 0.21875
- query_bias: bfloat16 [768], P(('dp', 'blk')), may hold values from -3 to 3
- value_bias: bfloat16 [768], P(('dp', 'blk')), may hold values from -3 to 3
- output_weight: bfloat16 [768, 768], P(('dp', 'blk')), may hold values from -0.875 to 0.875
- output_bias: bfloat16 [768], P(('dp', 'blk')), may hold values from -2.5 to 2.5
- feed_gain: bfloat16 [768], P(('dp', 'blk')), may hold values from 0.099609375 to 1.8984375
- feed_shift: bfloat16 [768], P(('dp', 'blk')), may hold values from -2.5 to 2.5
- expand_weight: bfloat16 [768, 3072], P(('dp', 'blk')), may hold values from -0.21875 to 0.21875
- expand_bias: bfloat16 [3072], P(('dp', 'blk')), may hold values from -2.5 to 2.5
- shrink_weight: bfloat16 [3072, 768], P(('dp', 'blk')), may hold values from -0.21875 to 0.21875
- shrink_bias: bfloat16 [768], P(('dp', 'blk')), may hold values from -2.5 to 2.5
- cotangent: bfloat16 [32, 1252, 768], P('dp', 'blk'), may hold values from -6 to 6
Outputs:
- result: bfloat16 [32, 1252, 768], P('dp', 'blk')
- tokens_grad: bfloat16 [32, 1252, 768], P('dp', 'blk')
- attend_gain_grad: float32 [768], P(('dp', 'blk'))
- attend_shift_grad: float32 [768], P(('dp', 'blk'))
- merged_weight_grad: float32 [768, 2304], P(('dp', 'blk'))
- query_bias_grad: float32 [768], P(('dp', 'blk'))
- value_bias_grad: float32 [768], P(('dp', 'blk'))
- output_weight_grad: float32 [768, 768], P(('dp', 'blk'))
- output_bias_grad: float32 [768], P(('dp', 'blk'))
- feed_gain_grad: float32 [768], P(('dp', 'blk'))
- feed_shift_grad: float32 [768], P(('dp', 'blk'))
- expand_weight_grad: float32 [768, 3072], P(('dp', 'blk'))
- expand_bias_grad: float32 [3072], P(('dp', 'blk'))
- shrink_weight_grad: float32 [3072, 768], P(('dp', 'blk'))
- shrink_bias_grad: float32 [768], P(('dp', 'blk'))
Inputs may be any that keep to these rules, and one draw needn't show every extreme that they name: `counts`: in every run of 2 clips that share an index of dp, one clip drawn from the seed has more than 52 columns; in the first run that clip has all 104.
All inputs are finite; a program needn't handle non-finite values.
Results may differ from a plain program's by a relative error of at most 0.017.
Values may be sent and summed in bfloat16 or wider, within the bound.
No kernel may reach another device: no remote copies, remote signals or barrier semaphores. Data moves between devices by JAX's collectives and lax.ppermute only.
A program may use at most 320 MiB of HBM per device.

v0:
```python
from functools import partial

import jax
import jax.numpy as jnp
from jax import lax
from jax.sharding import PartitionSpec as P

HEADS = 12
HEAD_DIM = 64
FREQ = 12


EPSILON = 1e-06
NEGATIVE = -1e30


def from_behind(block, axis, distance):
    devices = range(lax.axis_size(axis))
    route = [((i - distance) % len(devices), i) for i in devices]
    return lax.ppermute(block, axis, route)


def layer_norm(values, scale_row, shift_row):
    mean_row = jnp.mean(values, axis=-1, keepdims=True)
    centered = values - mean_row
    spread = jnp.mean(centered * centered, axis=-1, keepdims=True)
    return centered * lax.rsqrt(spread + EPSILON) * scale_row + shift_row


def outer_sum(left_side, right_side):
    return lax.dot_general(
        left_side, right_side, (((0,), (0,)), ((), ())), preferred_element_type=jnp.float32
    )


def times_transposed(left_side, right_side):
    return lax.dot_general(
        left_side, right_side, (((1,), (1,)), ((), ())), preferred_element_type=jnp.float32
    )


def column_sum(values):
    return jnp.sum(values.astype(jnp.float32), axis=0)


def to_heads(values, clips, rows_dev):
    return values.reshape(clips, rows_dev, HEADS, HEAD_DIM).transpose(0, 2, 1, 3)


def from_heads(values):
    clips, heads, rows_dev, head_dim = values.shape
    return values.transpose(0, 2, 1, 3).reshape(clips * rows_dev, heads * head_dim)


def valid_keys(counts, positions, rows_dev):
    owner_block = positions // rows_dev
    offset = positions % rows_dev
    column = owner_block * ((rows_dev - 2) // FREQ) + (offset - 2) // FREQ
    special = (offset < 2)[None, :]
    return jnp.where(special, (owner_block == 0)[None, :], column[None, :] < counts[:, None])


def block_grads(query_part, key_part, value_part, grad_part, logsum, delta, visible, factor):
    scores = (
        jnp.einsum("chqd,chkd->chqk", query_part, key_part, preferred_element_type=jnp.float32)
        * factor
    )
    attention = jnp.where(visible[:, None, None, :], jnp.exp(scores - logsum[..., None]), 0.0)
    grad_attention = jnp.einsum(
        "chqd,chkd->chqk", grad_part, value_part, preferred_element_type=jnp.float32
    )
    grad_scores = (attention * (grad_attention - delta[..., None])).astype(jnp.bfloat16)
    grad_query = (
        jnp.einsum("chqk,chkd->chqd", grad_scores, key_part, preferred_element_type=jnp.float32)
        * factor
    )
    grad_keys = (
        jnp.einsum("chqk,chqd->chkd", grad_scores, query_part, preferred_element_type=jnp.float32)
        * factor
    )
    grad_values = jnp.einsum(
        "chqk,chqd->chkd",
        attention.astype(jnp.bfloat16),
        grad_part,
        preferred_element_type=jnp.float32,
    )
    return (grad_query, grad_keys, grad_values)


def local(
    tokens,
    counts,
    attend_gain,
    attend_shift,
    merged_weight,
    query_bias,
    value_bias,
    output_weight,
    output_bias,
    feed_gain,
    feed_shift,
    expand_weight,
    expand_bias,
    shrink_weight,
    shrink_bias,
    cotangent,
):
    clips, rows_dev, width = tokens.shape
    total_rows = clips * rows_dev
    factor = HEAD_DIM ** (-0.5)
    cycle_size = lax.axis_size("blk")
    cycle_index = lax.axis_index("blk")
    shape_heads = (clips, HEADS, rows_dev, HEAD_DIM)
    shape_stats = (clips, HEADS, rows_dev)
    inputs = tokens.reshape(total_rows, width).astype(jnp.float32)
    attend_full = (
        lax.all_gather(attend_gain, ("dp", "blk"), axis=0, tiled=True),
        lax.all_gather(attend_shift, ("dp", "blk"), axis=0, tiled=True),
        lax.all_gather(merged_weight, ("dp", "blk"), axis=0, tiled=True),
        lax.all_gather(query_bias, ("dp", "blk"), axis=0, tiled=True),
        lax.all_gather(value_bias, ("dp", "blk"), axis=0, tiled=True),
        lax.all_gather(output_weight, ("dp", "blk"), axis=0, tiled=True),
        lax.all_gather(output_bias, ("dp", "blk"), axis=0, tiled=True),
    )
    attend_input = layer_norm(
        inputs, attend_full[0].astype(jnp.float32), attend_full[1].astype(jnp.float32)
    ).astype(jnp.bfloat16)
    merged_rows = jnp.dot(attend_input, attend_full[2], preferred_element_type=jnp.float32)
    query_rows = (merged_rows[:, :width] + attend_full[3]).astype(jnp.bfloat16)
    key_rows = merged_rows[:, width : 2 * width].astype(jnp.bfloat16)
    value_rows = (merged_rows[:, 2 * width :] + attend_full[4]).astype(jnp.bfloat16)
    query_heads = to_heads(query_rows, clips, rows_dev)
    key_heads = to_heads(key_rows, clips, rows_dev)
    value_heads = to_heads(value_rows, clips, rows_dev)
    row_top = jnp.full(shape_stats, NEGATIVE, jnp.float32)
    visit_key_part = lax.all_gather(key_heads, "blk", axis=2, tiled=True)
    visit_value_part = lax.all_gather(value_heads, "blk", axis=2, tiled=True)
    count_rows = visit_key_part.shape[2]
    visit_visible = valid_keys(counts, jnp.arange(count_rows, dtype=jnp.int32), rows_dev)[
        :, None, None, :
    ]
    scores = (
        jnp.einsum(
            "chqd,chkd->chqk", query_heads, visit_key_part, preferred_element_type=jnp.float32
        )
        * factor
    )
    scores = jnp.where(visit_visible, scores, NEGATIVE)
    new_top = jnp.maximum(row_top, jnp.max(scores, axis=-1))
    raised = jnp.where(visit_visible, jnp.exp(scores - new_top[..., None]), 0.0)
    row_total = jnp.sum(raised, axis=-1)
    mixture = jnp.einsum(
        "chqk,chkd->chqd",
        raised.astype(jnp.bfloat16),
        visit_value_part,
        preferred_element_type=jnp.float32,
    )
    row_top, row_total, mixture = (new_top, row_total, mixture)
    logsum = row_top + jnp.log(row_total)
    mixture_norm = mixture / row_total[..., None]
    attended = from_heads(mixture_norm).astype(jnp.bfloat16)
    middle = (
        inputs
        + jnp.dot(attended, attend_full[5], preferred_element_type=jnp.float32)
        + attend_full[6]
    )
    feed_full = (
        lax.all_gather(feed_gain, ("dp", "blk"), axis=0, tiled=True),
        lax.all_gather(feed_shift, ("dp", "blk"), axis=0, tiled=True),
        lax.all_gather(expand_weight, ("dp", "blk"), axis=0, tiled=True),
        lax.all_gather(expand_bias, ("dp", "blk"), axis=0, tiled=True),
        lax.all_gather(shrink_weight, ("dp", "blk"), axis=0, tiled=True),
        lax.all_gather(shrink_bias, ("dp", "blk"), axis=0, tiled=True),
    )
    feed_input = layer_norm(
        middle, feed_full[0].astype(jnp.float32), feed_full[1].astype(jnp.float32)
    ).astype(jnp.bfloat16)
    preact = jnp.dot(feed_input, feed_full[2], preferred_element_type=jnp.float32) + feed_full[3]
    hidden_float, gelu_pull = jax.vjp(partial(jax.nn.gelu, approximate=False), preact)
    hidden = hidden_float.astype(jnp.bfloat16)
    output_rows = (
        middle + jnp.dot(hidden, feed_full[4], preferred_element_type=jnp.float32) + feed_full[5]
    )
    result = output_rows.astype(jnp.bfloat16).reshape(clips, rows_dev, width)
    grad_rows = cotangent.reshape(total_rows, width)
    shrink_weight_grad = outer_sum(hidden, grad_rows)
    shrink_bias_grad = column_sum(grad_rows)
    grad_hidden = times_transposed(grad_rows, feed_full[4])
    grad_preact = gelu_pull(grad_hidden)[0].astype(jnp.bfloat16)
    expand_weight_grad = outer_sum(feed_input, grad_preact)
    expand_bias_grad = column_sum(grad_preact)
    grad_feed_input = times_transposed(grad_preact, feed_full[2])
    _, feed_pull = jax.vjp(
        layer_norm, middle, feed_full[0].astype(jnp.float32), feed_full[1].astype(jnp.float32)
    )
    grad_middle_norm, feed_gain_grad, feed_shift_grad = feed_pull(grad_feed_input)
    feed_terms = (
        feed_gain_grad,
        feed_shift_grad,
        expand_weight_grad,
        expand_bias_grad,
        shrink_weight_grad,
        shrink_bias_grad,
    )
    feed_summed = (
        lax.psum_scatter(feed_terms[0], ("dp", "blk"), scatter_dimension=0, tiled=True),
        lax.psum_scatter(feed_terms[1], ("dp", "blk"), scatter_dimension=0, tiled=True),
        lax.psum_scatter(feed_terms[2], ("dp", "blk"), scatter_dimension=0, tiled=True),
        lax.psum_scatter(feed_terms[3], ("dp", "blk"), scatter_dimension=0, tiled=True),
        lax.psum_scatter(feed_terms[4], ("dp", "blk"), scatter_dimension=0, tiled=True),
        lax.psum_scatter(feed_terms[5], ("dp", "blk"), scatter_dimension=0, tiled=True),
    )
    grad_middle = grad_rows.astype(jnp.float32) + grad_middle_norm
    grad_branch = grad_middle.astype(jnp.bfloat16)
    output_weight_grad = outer_sum(attended, grad_branch)
    output_bias_grad = column_sum(grad_branch)
    grad_attended = times_transposed(grad_branch, attend_full[5]).astype(jnp.bfloat16)
    grad_heads = to_heads(grad_attended, clips, rows_dev)
    delta = jnp.sum(grad_heads.astype(jnp.float32) * mixture_norm, axis=-1)
    grad_query = jnp.zeros(shape_heads, jnp.float32)
    travel = (
        key_heads,
        value_heads,
        jnp.zeros(shape_heads, jnp.float32),
        jnp.zeros(shape_heads, jnp.float32),
    )
    for turn_index in range(cycle_size):
        key_part, value_part, key_total, value_total = travel
        holder = (cycle_index - turn_index) % cycle_size
        visible = valid_keys(
            counts, holder * rows_dev + jnp.arange(rows_dev, dtype=jnp.int32), rows_dev
        )
        part_query, part_keys, part_values = block_grads(
            query_heads, key_part, value_part, grad_heads, logsum, delta, visible, factor
        )
        grad_query = grad_query + part_query
        key_total = key_total + part_keys
        value_total = value_total + part_values
        if turn_index + 1 < cycle_size:
            travel = (
                from_behind(key_part, "blk", 1),
                from_behind(value_part, "blk", 1),
                from_behind(key_total.astype(jnp.bfloat16), "blk", 1).astype(key_total.dtype),
                from_behind(value_total.astype(jnp.bfloat16), "blk", 1).astype(value_total.dtype),
            )
        else:
            grad_keys, grad_values = (
                from_behind(key_total.astype(jnp.bfloat16), "blk", 1).astype(key_total.dtype),
                from_behind(value_total.astype(jnp.bfloat16), "blk", 1).astype(value_total.dtype),
            )
    query_low = from_heads(grad_query).astype(jnp.bfloat16)
    keys_low = from_heads(grad_keys).astype(jnp.bfloat16)
    values_low = from_heads(grad_values).astype(jnp.bfloat16)
    query_bias_grad = column_sum(query_low)
    value_bias_grad = column_sum(values_low)
    merged_weight_grad = jnp.concatenate(
        [
            outer_sum(attend_input, query_low),
            outer_sum(attend_input, keys_low),
            outer_sum(attend_input, values_low),
        ],
        axis=1,
    )
    merged_full = attend_full[2]
    grad_attend_input = (
        times_transposed(query_low, merged_full[:, :width])
        + times_transposed(keys_low, merged_full[:, width : 2 * width])
        + times_transposed(values_low, merged_full[:, 2 * width :])
    )
    _, attend_pull = jax.vjp(
        layer_norm, inputs, attend_full[0].astype(jnp.float32), attend_full[1].astype(jnp.float32)
    )
    grad_inputs_norm, attend_gain_grad, attend_shift_grad = attend_pull(grad_attend_input)
    attend_terms = (
        attend_gain_grad,
        attend_shift_grad,
        merged_weight_grad,
        query_bias_grad,
        value_bias_grad,
        output_weight_grad,
        output_bias_grad,
    )
    attend_summed = (
        lax.psum_scatter(attend_terms[0], ("dp", "blk"), scatter_dimension=0, tiled=True),
        lax.psum_scatter(attend_terms[1], ("dp", "blk"), scatter_dimension=0, tiled=True),
        lax.psum_scatter(attend_terms[2], ("dp", "blk"), scatter_dimension=0, tiled=True),
        lax.psum_scatter(attend_terms[3], ("dp", "blk"), scatter_dimension=0, tiled=True),
        lax.psum_scatter(attend_terms[4], ("dp", "blk"), scatter_dimension=0, tiled=True),
        lax.psum_scatter(attend_terms[5], ("dp", "blk"), scatter_dimension=0, tiled=True),
        lax.psum_scatter(attend_terms[6], ("dp", "blk"), scatter_dimension=0, tiled=True),
    )
    tokens_grad = (
        (grad_middle + grad_inputs_norm).astype(jnp.bfloat16).reshape(clips, rows_dev, width)
    )
    return (
        result,
        tokens_grad,
        attend_summed[0],
        attend_summed[1],
        attend_summed[2],
        attend_summed[3],
        attend_summed[4],
        attend_summed[5],
        attend_summed[6],
        feed_summed[0],
        feed_summed[1],
        feed_summed[2],
        feed_summed[3],
        feed_summed[4],
        feed_summed[5],
    )


def solution(mesh):
    in_specs = (
        P("dp", "blk", None),
        P("dp"),
        P(("dp", "blk")),
        P(("dp", "blk")),
        P(("dp", "blk"), None),
        P(("dp", "blk")),
        P(("dp", "blk")),
        P(("dp", "blk"), None),
        P(("dp", "blk")),
        P(("dp", "blk")),
        P(("dp", "blk")),
        P(("dp", "blk"), None),
        P(("dp", "blk")),
        P(("dp", "blk"), None),
        P(("dp", "blk")),
        P("dp", "blk", None),
    )
    out_specs = (
        P("dp", "blk", None),
        P("dp", "blk", None),
        P(("dp", "blk")),
        P(("dp", "blk")),
        P(("dp", "blk"), None),
        P(("dp", "blk")),
        P(("dp", "blk")),
        P(("dp", "blk"), None),
        P(("dp", "blk")),
        P(("dp", "blk")),
        P(("dp", "blk")),
        P(("dp", "blk"), None),
        P(("dp", "blk")),
        P(("dp", "blk"), None),
        P(("dp", "blk")),
    )
    return jax.shard_map(local, mesh=mesh, in_specs=in_specs, out_specs=out_specs, check_vma=False)
```

profile of v0, /device:TPU:0, one launch (start us, length us, event | category | flops | bytes accessed | tf_op | source)
XLA Modules:
  0.0 902.5 jit_solution(17864525211978495949)
XLA Ops:
  15.5 42.8 %all-reduce.19 = (bf16[768]{0:T(1024)(128)(2,1)S(1)}, bf16[768]{0:T(1024)(128)(2,1)S(1)}, bf16[768]{0:T(1024)(128)(2,1)S(1)}, bf16[768]{0:T(1024)(128)(2,1)S(1)}...) all-reduce(bf16[768]{0:T(1024)(128)(2,1)S(1)} %dynamic-update-slice, ...), channel_id=1, replica_groups=mesh['dp'=16,'blk'=2] {'dp','blk'}, use_global_device_ids=true, to_apply=%add.1 | all-reduce | flops 9216 | bytes 36864
  147.7 30.9 %fusion = (f32[2,12,626]{2,1,0:T(8,128)S(1)}, f32[2,12,626,1252]{2,3,1,0:T(8,128)}) fusion(pred[2,1252]{1,0:T(4,128)(4,1)S(1)} %compare_select_fusion, bf16[2,12,1252,64]{3,0,1,2:T(2,128)(2,1)} %all-gather.9.cloned.1.call-done, bf16[2,12,626,64]{2,0,3,1:T(2,128)(2,1)S(1)} %bitcast.84), kind=kOutput, calls=%fused_computation.2 | convolution fusion | flops 2464101376 | bytes 81072008 | tf_op jit(solution)/shard_map/chqd,chkd->chqk/dot_general | solution.py:143
  178.6 27.0 %fusion.1 = f32[2,12,626]{2,1,0:T(8,128)S(1)} fusion(f32[2,12,626,1252]{2,3,1,0:T(8,128)} %get-tuple-element.114, f32[2,12,626]{2,1,0:T(8,128)S(1)} %broadcast_maximum_fusion, pred[2,1252]{1,0:T(4,128)(4,1)S(1)} %compare_select_fusion), kind=kLoop, calls=%fused_computation.3 | loop fusion | flops 94035216 | bytes 75362888 | tf_op jit(solution)/shard_map/reduce_sum | solution.py:151
  205.6 44.0 %fusion.23 = (bf16[2,626,12,64]{1,3,2,0:T(8,128)(2,1)}, f32[2,12,626,64]{2,3,1,0:T(8,128)}) fusion(f32[2,626,12]{1,2,0:T(8,128)S(1)} %bitcast.89, bf16[2,12,1252,64]{3,0,1,2:T(2,128)(2,1)} %all-gather.11.cloned.1.call-done, f32[2,12,626,1252]{2,3,1,0:T(8,128)} %get-tuple-element.114, f32[2,12,626]{2,1,0:T(8,128)S(1)} %broadcast_maximum_fusion, ...), kind=kOutput, calls=%fused_computation.42 | convolution fusion | flops 2503659520 | bytes 84978248 | tf_op jit(solution)/shard_map/chqk,chkd->chqd/dot_general | solution.py:152
  263.7 12.3 %all-gather.15.cloned.1.call-done = bf16[768,3072]{1,0:T(8,128)(2,1)} async-done(((bf16[24,3072]{1,0:T(8,128)(2,1)}), bf16[768,3072]{1,0:T(8,128)(2,1)}) %all-gather.15.cloned.1.call-update) | async-done | bytes 4718608 | tf_op jit(solution)/shard_map/all_gather | solution.py:170
  275.9 46.0 %multiply_convert_fusion.2 = (bf16[1252,3072]{1,0:T(8,128)(2,1)}, f32[1252,3072]{1,0:T(8,128)}, f32[1252,3072]{1,0:T(8,128)}) fusion(f32[3072]{0:T(1024)S(1)} %convert_element_type.193, bf16[768,3072]{1,0:T(8,128)(2,1)} %all-gather.15.cloned.1.call-done, f32[1252,768]{1,0:T(8,128)} %copy-done.12, f32[768]{0:T(1024)S(1)} %convert_element_type.191, ...), kind=kOutput, calls=%fused_computation.21 | convolution fusion | flops 6166330368 | bytes 47054624 | tf_op jit(solution)/shard_map/dot_general | solution.py:178
  322.0 19.2 %all-gather.17.cloned.1.call-done = bf16[3072,768]{1,0:T(8,128)(2,1)} async-done(((bf16[96,768]{1,0:T(8,128)(2,1)}), bf16[3072,768]{1,0:T(8,128)(2,1)}) %all-gather.17.cloned.1.call-update) | async-done | bytes 4718608 | tf_op jit(solution)/shard_map/all_gather | solution.py:172
  341.1 20.2 %convert_reduce_fusion = (f32[3072]{0:T(1024)}, bf16[1252,3072]{1,0:T(8,128)(2,1)}) fusion(f32[1252,3072]{1,0:T(8,128)} %get-tuple-element.106, bf16[1252,768]{1,0:T(8,128)(2,1)S(1)} %copy-done.8, bf16[3072,768]{1,0:T(8,128)(2,1)} %all-gather.17.cloned.1.call-done, f32[1252,3072]{1,0:T(8,128)} %get-tuple-element.119, f32[3072]{0:T(1024)S(1)} %convert_element_type.193), kind=kOutput, calls=%fused_computation.19 | convolution fusion | flops 5973058560 | bytes 45127680 | tf_op jit(solution)/shard_map/dot_general | solution.py:37
  361.3 12.6 %multiply_reduce_fusion.1 = (f32[768]{0:T(1024)}, f32[1252]{0:T(1024)S(1)}, f32[768]{0:T(1024)}, f32[1252,768]{1,0:T(8,128)S(1)}) fusion(f32[1252,768]{1,0:T(8,128)} %copy-done.12, f32[1252]{0:T(1024)S(1)} %fusion.73, f32[1252]{0:T(1024)S(1)} %broadcast_multiply_fusion.1, f32[768]{0:T(1024)S(1)} %convert_element_type.190, ...), kind=kOutput, calls=%fused_computation.61 | convolution fusion | flops 5915366400 | bytes 20127408 | tf_op jit(solution)/shard_map/dot_general | solution.py:37
  390.3 12.9 %fusion.101 = f32[768,3072]{1,0:T(8,128)} fusion(bf16[1252,3072]{1,0:T(8,128)(2,1)} %get-tuple-element.125, f32[1252,768]{1,0:T(8,128)} %copy-done.12, f32[768]{0:T(1024)S(1)} %convert_element_type.191, f32[768]{0:T(1024)S(1)} %convert_element_type.190, f32[1252]{0:T(1024)S(1)} %fusion.73, f32[1252]{0:T(1024)S(1)} %broadcast_multiply_fusion.1), kind=kOutput, calls=%fused_computation.181 | convolution fusion | flops 5912484864 | bytes 20991776 | tf_op jit(solution)/shard_map/dot_general | solution.py:31
  404.8 17.4 %fusion.61 = f32[2,12,626,626]{3,2,1,0:T(8,128)} fusion(bf16[2,12,626,64]{2,0,3,1:T(2,128)(2,1)S(1)} %bitcast.85, bf16[2,626,12,64]{1,0,3,2:T(2,128)(2,1)} %copy-done.2), kind=kOutput, calls=%fused_computation.103 | convolution fusion | flops 1203843072 | bytes 41466240 | tf_op jit(solution)/shard_map/chqd,chkd->chqk/dot_general | solution.py:65
  422.2 17.3 %fusion.59 = f32[2,12,626,626]{3,2,1,0:T(8,128)} fusion(bf16[2,12,626,64]{2,3,1,0:T(8,128)(2,1)} %collective-permute-done, bf16[2,12,626,64]{2,0,3,1:T(2,128)(2,1)S(1)} %bitcast.86), kind=kOutput, calls=%fused_computation.101 | convolution fusion | flops 1203843072 | bytes 41466240 | tf_op jit(solution)/shard_map/chqd,chkd->chqk/dot_general | solution.py:65
  452.4 19.9 %fusion.39 = bf16[2,12,626,64]{2,3,1,0:T(8,128)(2,1)} fusion(f32[2,12,626,626]{3,2,1,0:T(8,128)} %fusion.61, f32[2,12,626]{2,1,0:T(8,128)S(1)} %log_add_fusion, pred[2,626]{1,0:T(4,128)(4,1)S(1)} %get-tuple-element.112, bf16[2,626,12,64]{1,0,3,2:T(2,128)(2,1)} %reshape.464), kind=kOutput, calls=%fused_computation.89 | convolution fusion | flops 1242424704 | bytes 41527588 | tf_op jit(solution)/shard_map/chqk,chqd->chkd/dot_general | solution.py:81
  473.8 23.7 %multiply_convert_fusion.1 = bf16[2,12,626,626]{3,2,1,0:T(8,128)(2,1)} fusion(f32[2,12,626,626]{3,2,1,0:T(8,128)} %fusion.61, f32[2,12,626]{2,1,0:T(8,128)S(1)} %multiply_reduce_fusion, f32[2,12,626]{2,1,0:T(8,128)S(1)} %log_add_fusion, pred[2,626]{1,0:T(4,128)(4,1)S(1)} %get-tuple-element.112, bf16[2,626,12,64]{1,0,3,2:T(2,128)(2,1)S(1)} %copy-done.16, ...), kind=kOutput, calls=%fused_computation.7 | convolution fusion | flops 1260273280 | bytes 60397732 | tf_op jit(solution)/shard_map/chqd,chkd->chqk/dot_general | solution.py:69
  497.5 11.1 %fusion.112 = f32[3072,768]{1,0:T(8,128)} fusion(bf16[1252,3072]{1,0:T(8,128)(2,1)} %get-tuple-element.105, bf16[1252,768]{1,0:T(8,128)(2,1)S(1)} %copy-done.9), kind=kOutput, calls=%fused_computation.190 | convolution fusion | flops 5907677184 | bytes 19052544 | tf_op jit(solution)/shard_map/dot_general | solution.py:31
  508.6 10.5 %multiply_convert_fusion.3 = bf16[2,12,626,64]{2,3,1,0:T(8,128)(2,1)} fusion(bf16[2,12,626,626]{3,2,1,0:T(8,128)(2,1)} %multiply_convert_fusion.1, bf16[2,12,626,64]{2,0,3,1:T(2,128)(2,1)S(1)} %bitcast.87), kind=kOutput, calls=%fused_computation.47 | convolution fusion | flops 1205766144 | bytes 22656192 | tf_op jit(solution)/shard_map/chqk,chqd->chkd/dot_general | solution.py:78
  519.4 26.2 %multiply_convert_fusion = bf16[2,12,626,626]{3,2,1,0:T(8,128)(2,1)} fusion(f32[2,12,626,626]{3,2,1,0:T(8,128)} %fusion.59, f32[2,12,626]{2,1,0:T(8,128)S(1)} %multiply_reduce_fusion, f32[2,12,626]{2,1,0:T(8,128)S(1)} %log_add_fusion, pred[2,626]{1,0:T(4,128)(4,1)S(1)} %copy-done.56, bf16[2,12,626,64]{2,3,1,0:T(8,128)(2,1)} %collective-permute-done.1, ...), kind=kOutput, calls=%fused_computation.5 | convolution fusion | flops 1260273280 | bytes 60397732 | tf_op jit(solution)/shard_map/chqd,chkd->chqk/dot_general | solution.py:69
  545.7 16.7 %add_convert_fusion.1 = bf16[2,12,626,64]{2,3,1,0:T(8,128)(2,1)} fusion(bf16[2,12,626,64]{2,3,1,0:T(8,128)(2,1)} %collective-permute-done.4, f32[2,12,626,626]{3,2,1,0:T(8,128)} %fusion.59, f32[2,12,626]{2,1,0:T(8,128)S(1)} %log_add_fusion, pred[2,626]{1,0:T(4,128)(4,1)S(1)} %copy-done.56, bf16[2,626,12,64]{1,0,3,2:T(2,128)(2,1)S(1)} %copy-done.17), kind=kOutput, calls=%fused_computation.45 | convolution fusion | flops 1244347776 | bytes 43450660 | tf_op jit(solution)/shard_map/chqk,chqd->chkd/dot_general | solution.py:81
  572.9 10.3 %fusion.100 = f32[2,12,626,64]{2,3,1,0:T(8,128)S(1)} fusion(bf16[2,12,626,626]{3,2,1,0:T(8,128)(2,1)} %multiply_convert_fusion.1, bf16[2,626,12,64]{1,0,3,2:T(2,128)(2,1)S(1)} %copy-done.3), kind=kOutput, calls=%fused_computation.180 | convolution fusion | flops 1203843072 | bytes 24579264 | tf_op jit(solution)/shard_map/chqk,chkd->chqd/dot_general | solution.py:74
  583.2 11.0 %convert_reduce_fusion.2 = (f32[12,64]{1,0:T(8,128)S(1)}, bf16[2,626,12,64]{1,3,2,0:T(8,128)(2,1)S(1)}) fusion(f32[2,12,626,64]{2,3,1,0:T(8,128)S(1)} %fusion.100, bf16[2,12,626,626]{3,2,1,0:T(8,128)(2,1)} %multiply_convert_fusion, bf16[2,12,626,64]{2,3,1,0:T(8,128)(2,1)} %collective-permute-done), kind=kOutput, calls=%fused_computation.44 | convolution fusion | flops 1208649984 | bytes 26505408 | tf_op jit(solution)/shard_map/chqk,chkd->chqd/dot_general | solution.py:74
  640.6 12.1 %fusion.28 = bf16[1252,768]{1,0:T(8,128)(2,1)} fusion(f32[1252,768]{1,0:T(8,128)} %copy-done.12, bf16[1252,3072]{1,0:T(8,128)(2,1)} %get-tuple-element.105, bf16[3072,768]{1,0:T(8,128)(2,1)} %all-gather.17.cloned.1.call-done, f32[768]{0:T(1024)S(1)} %convert_element_type.195), kind=kOutput, calls=%fused_computation.74 | convolution fusion | flops 5910561792 | bytes 18183168 | tf_op jit(solution)/shard_map/dot_general | solution.py:182
  675.6 43.8 %all-reduce.18 = (f32[768]{0:T(1024)S(1)}, f32[768]{0:T(1024)S(1)}, f32[768]{0:T(1024)S(1)}, f32[768]{0:T(1024)S(1)}, f32[768]{0:T(1024)S(1)}, /*index=5*/f32[76...) all-reduce(f32[768]{0:T(1024)S(1)} %get-tuple-element.77, ...), channel_id=2, replica_groups=mesh['dp'=16,'blk'=2] {'dp','blk'}, use_global_device_ids=true, to_apply=%region_12.13.clone | all-reduce | flops 9216 | bytes 73728
  736.6 33.2 %reduce-scatter.11.cloned.1.call-done = f32[96,768]{1,0:T(8,128)} async-done(((f32[3072,768]{1,0:T(8,128)}), f32[96,768]{1,0:T(8,128)}) %reduce-scatter.11.cloned.1.call-update) | async-done | bytes 294928 | tf_op jit(solution)/shard_map/reduce_scatter | solution.py:210
  769.9 125.3 %reduce-scatter.13.cloned.1.call-done = f32[24,2304]{1,0:T(8,128)} async-done(((f32[768,2304]{1,0:T(8,128)}), f32[24,2304]{1,0:T(8,128)}) %reduce-scatter.13.cloned.1.call-update) | async-done | bytes 221200
  (277 shorter events, 240.6 us)
Async XLA Ops:
  7.2 54.8 %copy-start.6 = (bf16[2,626,768]{2,0,1:T(2,128)(2,1)S(1)}, bf16[2,626,768]{2,0,1:T(2,128)(2,1)}, u32[]{:S(2)}) copy-start(bf16[2,626,768]{2,0,1:T(2,128)(2,1)} %param.16) | copy-start | bytes 5769220
  7.2 70.7 %all-gather.7.cloned.1.call-start = ((), (), s32[]{:S(2)}) async-start(), calls=%async_computation.4 | async-start | bytes 3649536 | tf_op jit(solution)/shard_map/all_gather | solution.py:119
  7.9 139.8 %all-gather.9.cloned.1.call-start = ((), (), s32[]{:S(2)}) async-start(), calls=%async_computation.5 | async-start | bytes 11538432 | tf_op jit(solution)/shard_map/all_gather | solution.py:136
  108.6 97.0 %all-gather.11.cloned.1.call-start = ((), (), s32[]{:S(2)}) async-start(), calls=%async_computation.6 | async-start | bytes 11538432 | tf_op jit(solution)/shard_map/all_gather | solution.py:137
  133.2 122.7 %all-gather.13.cloned.1.call-start = ((), (), s32[]{:S(2)}) async-start(), calls=%async_computation.7 | async-start | bytes 1216512 | tf_op jit(solution)/shard_map/all_gather | solution.py:122
  133.8 142.2 %all-gather.15.cloned.1.call-start = ((), (), s32[]{:S(2)}) async-start(), calls=%async_computation.8 | async-start | bytes 4866048 | tf_op jit(solution)/shard_map/all_gather | solution.py:170
  134.4 206.8 %all-gather.17.cloned.1.call-start = ((), (), s32[]{:S(2)}) async-start(), calls=%async_computation.9 | async-start | bytes 4866048 | tf_op jit(solution)/shard_map/all_gather | solution.py:172
  134.9 601.7 %reduce-scatter.7.cloned.1.call-start = ((), (), s32[]{:S(2)}) async-start(), calls=%async_computation.10 | async-start | bytes 2433024 | tf_op jit(solution)/shard_map/reduce_scatter | solution.py:289
  147.7 30.9 %copy-start = (bf16[2,626,12,64]{1,0,3,2:T(2,128)(2,1)}, bf16[2,626,12,64]{1,0,3,2:T(2,128)(2,1)S(1)}, u32[]{:S(2)}) copy-start(bf16[2,626,12,64]{1,0,3,2:T(2,128)(2,1)S(1)} %reshape.459) | copy-start | bytes 5769220
  178.6 27.0 %copy-start.32 = (f32[2,12,626]{2,1,0:T(8,128)}, f32[2,12,626]{2,1,0:T(8,128)S(1)}, u32[]{:S(2)}) copy-start(f32[2,12,626]{2,1,0:T(8,128)S(1)} %get-tuple-element.113) | copy-start | bytes 180292
  205.6 44.1 %copy-start.34 = (f32[2,12,626]{2,1,0:T(8,128)}, f32[2,12,626]{2,1,0:T(8,128)S(1)}, u32[]{:S(2)}) copy-start(f32[2,12,626]{2,1,0:T(8,128)S(1)} %fusion.1) | copy-start | bytes 180292
  263.7 77.5 %copy-start.8 = (bf16[1252,768]{1,0:T(8,128)(2,1)S(1)}, bf16[1252,768]{1,0:T(8,128)(2,1)}, u32[]{:S(2)}) copy-start(bf16[1252,768]{1,0:T(8,128)(2,1)} %reshape.463) | copy-start | bytes 5769220
  382.2 354.5 %reduce-scatter.9.cloned.1.call-start = ((), (), s32[]{:S(2)}) async-start(), calls=%async_computation.11 | async-start | bytes 9732096 | tf_op jit(solution)/shard_map/reduce_scatter | solution.py:208
  389.8 32.4 %collective-permute-start = (bf16[2,12,626,64]{2,3,1,0:T(8,128)(2,1)}, bf16[2,12,626,64]{2,3,1,0:T(8,128)(2,1)}, u32[]{:S(2)}, u32[]{:S(2)}) collective-permute-start(bf16[2,12,626,64]{2,3,1,0:T(8,128)(2,1)} %bitcast.83), channel_id=1, source_target_pairs={{1,0},{0,1},{3,2},{2,3},{5,4},{4,5},{7,6},{6,7},{9,8},{8,9},{11,10... | collective-permute-start | bytes 5769224 | tf_op jit(solution)/shard_map/ppermute | solution.py:20
  390.1 129.3 %collective-permute-start.1 = (bf16[2,12,626,64]{2,3,1,0:T(8,128)(2,1)}, bf16[2,12,626,64]{2,3,1,0:T(8,128)(2,1)}, u32[]{:S(2)}, u32[]{:S(2)}) collective-permute-start(bf16[2,12,626,64]{2,3,1,0:T(8,128)(2,1)} %bitcast.82), channel_id=1, source_target_pairs={{1,0},{0,1},{3,2},{2,3},{5,4},{4,5},{7,6},{6,7},{9,8},{8,9},{11,10... | collective-permute-start | bytes 5769224 | tf_op jit(solution)/shard_map/ppermute | solution.py:20
  403.3 366.6 %reduce-scatter.11.cloned.1.call-start = ((), (), s32[]{:S(2)}) async-start(), calls=%async_computation.12 | async-start | bytes 9732096 | tf_op jit(solution)/shard_map/reduce_scatter | solution.py:210
  452.3 20.2 %copy-start.16 = (bf16[2,626,12,64]{1,0,3,2:T(2,128)(2,1)S(1)}, bf16[2,626,12,64]{1,0,3,2:T(2,128)(2,1)}, u32[]{:S(2)}) copy-start(bf16[2,626,12,64]{1,0,3,2:T(2,128)(2,1)} %reshape.464) | copy-start | bytes 5769220
  472.2 73.4 %collective-permute-start.4 = (bf16[2,12,626,64]{2,3,1,0:T(8,128)(2,1)}, bf16[2,12,626,64]{2,3,1,0:T(8,128)(2,1)}, u32[]{:S(2)}, u32[]{:S(2)}) collective-permute-start(bf16[2,12,626,64]{2,3,1,0:T(8,128)(2,1)} %fusion.39), channel_id=1, source_target_pairs={{1,0},{0,1},{3,2},{2,3},{5,4},{4,5},{7,6},{6,7},{9,8},{8,9},{11,10... | collective-permute-start | bytes 5769224 | tf_op jit(solution)/shard_map/ppermute | solution.py:20
  473.8 23.7 %copy-start.9 = (bf16[1252,768]{1,0:T(8,128)(2,1)S(1)}, bf16[1252,768]{1,0:T(8,128)(2,1)}, u32[]{:S(2)}) copy-start(bf16[1252,768]{1,0:T(8,128)(2,1)} %reshape.463) | copy-start | bytes 5769220
  508.6 386.6 %reduce-scatter.13.cloned.1.call-start = ((), (), s32[]{:S(2)}) async-start(), calls=%async_computation.13 | async-start | bytes 7299072
  519.2 43.5 %collective-permute-start.2 = (bf16[2,12,626,64]{2,3,1,0:T(8,128)(2,1)}, bf16[2,12,626,64]{2,3,1,0:T(8,128)(2,1)S(1)}, u32[]{:S(2)}, u32[]{:S(2)}) collective-permute-start(bf16[2,12,626,64]{2,3,1,0:T(8,128)(2,1)} %multiply_convert_fusion.3), channel_id=1, source_target_pairs={{1,0},{0,1},{3,2},{2,3},{5,4},{4,5},{7,6},{6,7},{9,8},{8,9},{11,10... | collective-permute-start | bytes 5769224 | tf_op jit(solution)/shard_map/ppermute | solution.py:20
  562.4 44.8 %collective-permute-start.5 = (bf16[2,12,626,64]{2,3,1,0:T(8,128)(2,1)}, bf16[2,12,626,64]{2,3,1,0:T(8,128)(2,1)}, u32[]{:S(2)}, u32[]{:S(2)}) collective-permute-start(bf16[2,12,626,64]{2,3,1,0:T(8,128)(2,1)} %add_convert_fusion.1), channel_id=1, source_target_pairs={{1,0},{0,1},{3,2},{2,3},{5,4},{4,5},{7,6},{6,7},{9,8},{8,9},{11,10... | collective-permute-start | bytes 5769224 | tf_op jit(solution)/shard_map/ppermute | solution.py:20
  572.7 40.7 %collective-permute-start.3 = (bf16[2,12,626,64]{2,3,1,0:T(8,128)(2,1)}, bf16[2,12,626,64]{2,3,1,0:T(8,128)(2,1)}, u32[]{:S(2)}, u32[]{:S(2)}) collective-permute-start(bf16[2,12,626,64]{2,3,1,0:T(8,128)(2,1)} %add_convert_fusion.2), channel_id=1, source_target_pairs={{1,0},{0,1},{3,2},{2,3},{5,4},{4,5},{7,6},{6,7},{9,8},{8,9},{11,10... | collective-permute-start | bytes 5769224 | tf_op jit(solution)/shard_map/ppermute | solution.py:20
  669.5 54.6 %copy-start.39 = (f32[1252]{0:T(1024)S(1)}, f32[1252]{0:T(1024)}, u32[]{:S(2)}) copy-start(f32[1252]{0:T(1024)} %copy-done.38) | copy-start | bytes 15028
  (53 other events, 338.6 us)
Sparse Core Ops, SparseCore 0:
  10.9 62.8 all-gather.6
  108.7 19.1 all-gather.8
  133.3 19.2 all-gather.10
  155.3 55.1 all-gather.12
  213.3 62.5 all-gather.14
  278.7 62.4 all-gather.16
  382.3 100.6 reduce-scatter.6
  490.5 136.6 reduce-scatter.8
  633.7 136.1 reduce-scatter.10
  776.9 118.2 reduce-scatter.12
where the time goes:
time: 914 us; the launch traced here: 903 us
  matrix products  400 us (44%)
  waiting for transfers between devices  192 us (21%)
  local copies, waits for them, and re-layouts  140 us (15%)
  blocking collectives  86.6 us (9%)
  other arithmetic  66.2 us (7%)
  between operations  15.5 us (2%)
    unnamed x11, waiting for transfers between devices  128 us
    unnamed x2, blocking collectives  86.6 us
    dot_general x6, matrix products, times_transposed(): lax.dot_general(left_side, right_side, (((1,), (1,)), ((), ())), preferre...  51.7 us
    dot_general x2, matrix products, block_grads(): jnp.einsum('chqd,chkd->chqk', grad_part, value_part, preferred_element_ty...  49.9 us
    dot_general x1, matrix products, local(): jnp.dot(feed_input, feed_full[2], preferred_element_type=jnp.float32)  46 us
    dot_general x1, matrix products, local(): jnp.einsum('chqk,chkd->chqd', raised.astype(jnp.bfloat16), visit_value_pa...  44 us
    unnamed x154, local copies, waits for them, and re-layouts  42.1 us
    dot_general x6, matrix products, outer_sum(): lax.dot_general(left_side, right_side, (((0,), (0,)), ((), ())), preferre...  38.4 us
  transfers between devices with their start and end apart: 16, of which 4 were waited for; matrix products, arithmetic and copies ran while one was open for 58% of the time, Pallas kernels for 0%

commit v1 on v0

v1 whole, which is shorter than its diff:
```python
from functools import partial

import jax
import jax.numpy as jnp
from jax import lax
from jax.experimental import pallas as pl
from jax.experimental.pallas import tpu as pltpu
from jax.sharding import PartitionSpec as P

HEADS = 12
HEAD_DIM = 64
FREQ = 12
EPSILON = 1e-06
NEGATIVE = -1e30
LOG2E = 1.4426950408889634
PAIRS = HEADS // 2
LANES = 2 * HEAD_DIM
ROW_GROUP = 8
VMEM_BYTES = 60 * 1024 * 1024

BF = jnp.bfloat16
F32 = jnp.float32

NN = (((1,), (0,)), ((), ()))
NT = (((1,), (1,)), ((), ()))
TN = (((0,), (0,)), ((), ()))


def dot(left, right, dims=NN):
    return lax.dot_general(left, right, dims, preferred_element_type=F32)


def params(count):
    return pltpu.CompilerParams(
        dimension_semantics=("arbitrary",) * count, vmem_limit_bytes=VMEM_BYTES
    )


def whole(shape):
    return pl.BlockSpec(shape, lambda *_: (0,) * len(shape), pipeline_mode=pl.Buffered(1))


def cost(flops, bytes_accessed, transcendentals=0):
    return pl.CostEstimate(
        flops=int(flops), bytes_accessed=int(bytes_accessed), transcendentals=int(transcendentals)
    )


def normed(values):
    mean_row = jnp.mean(values, axis=-1, keepdims=True)
    centered = values - mean_row
    spread = jnp.mean(centered * centered, axis=-1, keepdims=True)
    scale = lax.rsqrt(spread + EPSILON)
    return centered * scale, scale


def norm_back(upstream, gain_row, z, scale):
    w = upstream * gain_row
    return scale * (
        w - jnp.mean(w, axis=-1, keepdims=True) - z * jnp.mean(w * z, axis=-1, keepdims=True)
    )


def fold_rows(values):
    rows, width = values.shape
    return jnp.sum(values.reshape(rows // ROW_GROUP, ROW_GROUP, width), axis=0)


def row_tile(rows):
    return 256 if rows % 256 == 0 else rows


BITS_FIRST = (3, 2, 0, 1)
BITS_SECOND = (3, 2, 1, 0)


def quick_mesh(sizes):
    return sizes["dp"] == 16 and sizes["blk"] == 2


def swap_bit(block, bit):
    return lax.ppermute(block, "dp", [(i, i ^ (1 << bit)) for i in range(lax.axis_size("dp"))])


def sibling(block):
    return lax.ppermute(block, "blk", [(0, 1), (1, 0)])


def spread(block, bits):
    held = block[None]
    for bit in bits:
        held = jnp.concatenate([held, swap_bit(held, bit)], axis=0)
    return held


def relative(slot, bits):
    return sum(((slot >> k) & 1) << bit for k, bit in enumerate(bits))


def slot_of(offset, bits):
    return sum(((offset >> bit) & 1) << k for k, bit in enumerate(bits))


class Gathered:
    def __init__(self, shape, parts):
        self.shape = shape
        self.parts = parts

    @property
    def arrays(self):
        return [part[0] for part in self.parts]

    @property
    def copies(self):
        return sum(1 if bits is None else array.shape[0] for array, bits, _ in self.parts)

    def start(self, refs, target, sems):
        count = 0
        chip = lax.axis_index("dp")
        core = lax.axis_index("blk")
        for ref, (array, bits, place) in zip(refs, self.parts):
            if bits is None:
                pltpu.make_async_copy(ref, target, sems.at[count]).start()
                count += 1
                continue
            slots, rows, cols = array.shape
            for slot in range(slots):
                owner = lax.bitwise_xor(chip, jnp.int32(relative(slot, bits)))
                first_row, first_col = place(owner, core)
                spot = target.at[
                    pl.ds(pl.multiple_of(first_row, 16), rows),
                    pl.ds(pl.multiple_of(first_col, 128), cols),
                ]
                pltpu.make_async_copy(ref.at[slot], spot, sems.at[count]).start()
                count += 1

    def wait(self, refs, target, sems):
        count = 0
        for ref, (array, bits, _) in zip(refs, self.parts):
            if bits is None:
                pltpu.make_async_copy(ref, target, sems.at[count]).wait()
                count += 1
                continue
            slots, rows, cols = array.shape
            for slot in range(slots):
                spot = target.at[pl.ds(0, rows), pl.ds(0, cols)]
                pltpu.make_async_copy(ref.at[slot], spot, sems.at[count]).wait()
                count += 1


def gather_halves(block, cuts):
    rows, cols = block.shape
    half = cols // 2
    core = lax.axis_index("blk")
    mine = lax.dynamic_slice_in_dim(block, core * half, half, axis=1)
    other = sibling(lax.dynamic_slice_in_dim(block, (1 - core) * half, half, axis=1))
    chip_rows = jnp.where(
        core == 0,
        jnp.concatenate([mine, other], axis=0),
        jnp.concatenate([other, mine], axis=0),
    )
    parts = []
    start = 0
    for width, bits in cuts:
        held = spread(chip_rows[:, start : start + width], bits)

        def place(owner, which, start=start, flip=0):
            return owner * (2 * rows), (which ^ flip) * half + start

        parts.append((held, bits, place))
        parts.append((sibling(held), bits, partial(place, flip=1)))
        start += width
    return Gathered((32 * rows, cols), parts)


def gather_rows(block, bits):
    rows, cols = block.shape
    held = spread(block, bits)

    def place(owner, which, flip=0):
        return (owner * 2 + (which ^ flip)) * rows, 0

    parts = [(held, bits, place), (sibling(held), bits, partial(place, flip=1))]
    return Gathered((32 * rows, cols), parts)


def gather_plain(block):
    full = lax.all_gather(block, ("dp", "blk"), axis=0, tiled=True)
    return Gathered(full.shape, [(full, None, None)])


ANYWHERE = pl.BlockSpec(memory_space=pl.ANY)


VEC_COLS = 256


def project_body(*refs, weight):
    count = len(weight.parts)
    x_ref = refs[0]
    sources = refs[1 : 1 + count]
    a_ref, m_ref, w_ref, vec_ref, sems = refs[1 + count :]
    width = x_ref.shape[1]
    first = pl.program_id(0) == 0

    @pl.when(first)
    def _():
        weight.start(sources, w_ref, sems)

    z, _ = normed(x_ref[...].astype(F32))

    @pl.when(first)
    def _():
        weight.wait(sources, w_ref, sems)
        turned = jnp.transpose(w_ref[:, 3 * width : 3 * width + 128].astype(F32))
        vec_ref[...] = turned[:16]

    a = (z * vec_ref[0:1, :] + vec_ref[1:2, :]).astype(BF)
    a_ref[...] = a
    merged = dot(a, w_ref[:, : 3 * width])
    query = (merged[:, :width] + vec_ref[2:3, :]) * (LOG2E * HEAD_DIM**-0.5)
    m_ref[:, :width] = query.astype(BF)
    m_ref[:, width : 2 * width] = merged[:, width : 2 * width].astype(BF)
    m_ref[:, 2 * width :] = (merged[:, 2 * width :] + vec_ref[3:4, :]).astype(BF)


def project(x, weight):
    rows, width = x.shape
    tile = row_tile(rows)
    row = lambda cols: pl.BlockSpec((tile, cols), lambda i: (i, 0))
    return pl.pallas_call(
        partial(project_body, weight=weight),
        grid=(rows // tile,),
        in_specs=[row(width)] + [ANYWHERE] * len(weight.parts),
        out_specs=[row(width), row(3 * width), whole(weight.shape), whole((16, width))],
        out_shape=[
            jax.ShapeDtypeStruct((rows, width), BF),
            jax.ShapeDtypeStruct((rows, 3 * width), BF),
            jax.ShapeDtypeStruct(weight.shape, BF),
            jax.ShapeDtypeStruct((16, width), F32),
        ],
        scratch_shapes=[pltpu.SemaphoreType.DMA((weight.copies,))],
        compiler_params=params(1),
        cost_estimate=cost(6 * rows * width * width, 2 * rows * width * 5 + 6 * width * width),
        name="project",
    )(x, *weight.arrays)


def half_lanes(shape, head):
    return (lax.broadcasted_iota(jnp.int32, shape, 1) < HEAD_DIM) == (head == 0)


def only_head(values, head):
    return jnp.where(half_lanes(values.shape, head), values, jnp.zeros_like(values))


def ones_lane(rows):
    first = lax.broadcasted_iota(jnp.int32, (rows, LANES), 1) == 0
    return jnp.where(first, 1.0, 0.0).astype(BF)


def attend_body(q_ref, k_ref, v_ref, mask_ref, o_ref, sum_ref, *, tile):
    keys = k_ref.shape[1]
    queries = q_ref.shape[1]
    ka = jnp.concatenate([k_ref[0], mask_ref[0]], axis=1)
    v_turned = jnp.transpose(v_ref[0])
    ones = jnp.ones((16, keys), BF)
    va = [
        jnp.concatenate([v_turned[:HEAD_DIM], ones], axis=0),
        jnp.concatenate([v_turned[HEAD_DIM:], ones], axis=0),
    ]
    one = ones_lane(tile)
    for start in range(0, queries, tile):
        q = q_ref[0, start : start + tile, :]
        parts = []
        for head in range(2):
            qa = jnp.concatenate([only_head(q, head), one], axis=1)
            s = dot(ka, qa, NT)
            top = jnp.max(s, axis=0, keepdims=True)
            p = jnp.exp2(s - top).astype(BF)
            mix = dot(va[head], p)
            total = mix[HEAD_DIM : HEAD_DIM + 1]
            parts.append(mix[:HEAD_DIM] / total)
            sum_ref[0, head : head + 1, start : start + tile] = top + jnp.log2(total)
        o_ref[0, start : start + tile, :] = jnp.transpose(jnp.concatenate(parts, axis=0))


def attend(merged, key_merged, key_base, mask, first=0, count=PAIRS):
    clips, queries, _ = merged.shape
    keys = key_merged.shape[1]
    tile = row_tile(queries)
    lanes = lambda rows, base: pl.BlockSpec((1, rows, LANES), lambda c, h: (c, 0, base + h))
    return pl.pallas_call(
        partial(attend_body, tile=tile),
        grid=(clips, count),
        in_specs=[
            lanes(queries, first),
            lanes(keys, key_base + first),
            lanes(keys, key_base + PAIRS + first),
            pl.BlockSpec((1, keys, LANES), lambda c, h: (c, 0, 0)),
        ],
        out_specs=[
            lanes(queries, 0),
            pl.BlockSpec((1, ROW_GROUP, queries), lambda c, h: (c, h, 0)),
        ],
        out_shape=[
            jax.ShapeDtypeStruct((clips, queries, count * LANES), F32),
            jax.ShapeDtypeStruct((clips, count * ROW_GROUP, queries), F32),
        ],
        compiler_params=params(2),
        cost_estimate=cost(
            clips * count * queries * keys * 2 * 4 * 256,
            clips * count * LANES * (2 * queries + 4 * keys + 4 * queries),
            clips * count * queries * keys * 2,
        ),
        name="attend",
    )(merged, key_merged, key_merged, mask)


def attend_back_body(
    q_ref, k_ref, v_ref, do_ref, mask_ref, sum_ref, delta_ref, dq_ref, dk_ref, dv_ref,
    dk_acc, dv_acc, *, tile
):
    queries = q_ref.shape[1]
    k = k_ref[0]
    v = v_ref[0]
    ka = jnp.concatenate([k, mask_ref[0]], axis=1)
    k_turned = jnp.transpose(k)
    one = ones_lane(tile)
    for start in range(0, queries, tile):
        rows = slice(start, start + tile)
        q = q_ref[0, rows, :]
        do = do_ref[0, rows, :]
        q_parts, do_parts, p_parts, ds_parts, dq_parts = [], [], [], [], []
        for head in range(2):
            qm = only_head(q, head)
            dom = only_head(do, head)
            s = dot(ka, jnp.concatenate([qm, one], axis=1), NT)
            p = jnp.exp2(s - sum_ref[0, head : head + 1, rows])
            dp = dot(v, dom, NT)
            ds = (p * (dp - delta_ref[0, head : head + 1, rows])).astype(BF)
            q_parts.append(qm)
            do_parts.append(dom)
            p_parts.append(p.astype(BF))
            ds_parts.append(ds)
            dq_parts.append(dot(k_turned[head * HEAD_DIM : (head + 1) * HEAD_DIM], ds))
        dq = jnp.transpose(jnp.concatenate(dq_parts, axis=0)) * (HEAD_DIM**-0.5)
        dq_ref[0, rows, :] = dq.astype(BF)
        dk = dot(jnp.concatenate(ds_parts, axis=1), jnp.concatenate(q_parts, axis=0))
        dv = dot(jnp.concatenate(p_parts, axis=1), jnp.concatenate(do_parts, axis=0))
        if start == 0:
            dk_acc[...] = dk
            dv_acc[...] = dv
        else:
            dk_acc[...] += dk
            dv_acc[...] += dv
    dk_ref[0] = (dk_acc[...] * (1.0 / LOG2E)).astype(BF)
    dv_ref[0] = dv_acc[...].astype(BF)


def attend_back(merged, key_merged, key_base, grad_out, mask, sums, delta, first=0, count=PAIRS):
    clips, queries, _ = merged.shape
    keys = key_merged.shape[1]
    tile = row_tile(queries)
    lanes = lambda rows, base: pl.BlockSpec((1, rows, LANES), lambda c, h: (c, 0, base + h))
    stat = lambda base: pl.BlockSpec((1, ROW_GROUP, queries), lambda c, h: (c, base + h, 0))
    return pl.pallas_call(
        partial(attend_back_body, tile=tile),
        grid=(clips, count),
        in_specs=[
            lanes(queries, first),
            lanes(keys, key_base + first),
            lanes(keys, key_base + PAIRS + first),
            lanes(queries, first),
            pl.BlockSpec((1, keys, LANES), lambda c, h: (c, 0, 0)),
            stat(0),
            stat(first),
        ],
        out_specs=[lanes(queries, 0), lanes(keys, 0), lanes(keys, 0)],
        out_shape=[
            jax.ShapeDtypeStruct((clips, queries, count * LANES), BF),
            jax.ShapeDtypeStruct((clips, keys, count * LANES), BF),
            jax.ShapeDtypeStruct((clips, keys, count * LANES), BF),
        ],
        scratch_shapes=[pltpu.VMEM((keys, LANES), F32), pltpu.VMEM((keys, LANES), F32)],
        compiler_params=params(2),
        cost_estimate=cost(
            clips * count * queries * keys * 2 * 9 * 256,
            clips * count * LANES * 2 * (3 * queries + 4 * keys),
            clips * count * queries * keys * 2,
        ),
        name="attend_back",
    )(merged, key_merged, key_merged, grad_out, mask, sums, delta)


ERF = (0.254829592, -0.284496736, 1.421413741, -1.453152027, 1.061405429)
ERF_P = 0.3275911


def gelu_both(u):
    bell = jnp.exp2(u * u * (-0.5 * LOG2E))
    t = 1.0 / (1.0 + (ERF_P * 0.5**0.5) * jnp.abs(u))
    series = ERF[4] * 0.5
    for term in ERF[3::-1]:
        series = series * t + term * 0.5
    tail = series * t * bell
    chance = jnp.where(u >= 0, 1.0 - tail, tail)
    return u * chance, chance + u * bell * 0.3989422804014327


def feed_body(*refs, chunk, mixes, wide, tall):
    x_ref, g_ref = refs[:2]
    o_refs = refs[2 : 2 + mixes]
    at = 2 + mixes
    wide_refs = refs[at : at + len(wide.parts)]
    at += len(wide.parts)
    tall_refs = refs[at : at + len(tall.parts)]
    at += len(tall.parts)
    (
        vecs_ref, be_ref, sel_ref,
        result_ref, h_ref, gp_ref, gm_ref, att_ref, gb_ref, fi_ref, ga_ref, delta_ref, vec_ref,
        ebg_ref, wide_w, tall_w, wide_sems, tall_sems,
    ) = refs[at:]
    width = x_ref.shape[1]
    hidden_width = be_ref.shape[1]
    we_ref = wide_w.at[:, :hidden_width]
    wo_ref = wide_w.at[:, hidden_width:]
    ws_ref = tall_w

    @pl.when(pl.program_id(0) == 0)
    def _():
        wide.start(wide_refs, wide_w, wide_sems)
        tall.start(tall_refs, tall_w, tall_sems)
        vec_ref[...] = jnp.zeros_like(vec_ref)
        ebg_ref[...] = jnp.zeros_like(ebg_ref)
        wide.wait(wide_refs, wide_w, wide_sems)
        tall.wait(tall_refs, tall_w, tall_sems)

    o = jnp.concatenate([ref[...] for ref in o_refs], axis=1)
    att = o.astype(BF)
    att_ref[...] = att
    middle = x_ref[...].astype(F32) + dot(att, wo_ref[...]) + vecs_ref[4:5, :]
    z, scale = normed(middle)
    gain = vecs_ref[5:6, :]
    fi = (z * gain + vecs_ref[6:7, :]).astype(BF)
    fi_ref[...] = fi
    g = g_ref[...]
    out = middle + vecs_ref[7:8, :]
    u = jnp.zeros_like(middle)
    for start in range(0, hidden_width, chunk):
        cols = slice(start, start + chunk)
        pre = dot(fi, we_ref[:, cols]) + be_ref[:, cols]
        gh = dot(g, ws_ref[cols, :], NT)
        act, slope = gelu_both(pre)
        act = act.astype(BF)
        gp = (gh * slope).astype(BF)
        h_ref[:, cols] = act
        gp_ref[:, cols] = gp
        ebg_ref[:, cols] += fold_rows(gp.astype(F32))
        out += dot(act, ws_ref[cols, :])
        u += dot(gp, we_ref[:, cols], NT)
    result_ref[...] = out.astype(BF)
    gf = g.astype(F32)
    gm = gf + norm_back(u, gain, z, scale)
    gm_ref[...] = gm
    gb = gm.astype(BF)
    gb_ref[...] = gb
    ga = dot(gb, wo_ref[...], NT).astype(BF)
    ga_ref[...] = ga
    prod = ga.astype(F32) * o
    high = prod.astype(BF)
    low = (prod - high.astype(F32)).astype(BF)
    sel = sel_ref[...]
    delta_ref[...] = dot(sel, high, NT) + dot(sel, low, NT)
    vec_ref[:, :width] += fold_rows(u * z)
    vec_ref[:, width : 2 * width] += fold_rows(u)
    vec_ref[:, 2 * width : 3 * width] += fold_rows(gb.astype(F32))
    vec_ref[:, 3 * width :] += fold_rows(gf)


def feed(x, g, mixtures, wide, tall, vecs, be):
    rows, width = x.shape
    hidden_width = be.shape[1]
    tile = row_tile(rows)
    lane_head = jnp.arange(width)[None, :] // HEAD_DIM
    stat_row = jnp.arange(PAIRS * ROW_GROUP)[:, None]
    chosen = (stat_row // ROW_GROUP * 2 + stat_row % ROW_GROUP == lane_head) & (
        stat_row % ROW_GROUP < 2
    )
    select = chosen.astype(BF)
    row = lambda cols: pl.BlockSpec((tile, cols), lambda i: (i, 0))
    keep = lambda cols: pl.BlockSpec((ROW_GROUP, cols), lambda i: (0, 0))
    shape = jax.ShapeDtypeStruct
    return pl.pallas_call(
        partial(feed_body, chunk=512, mixes=len(mixtures), wide=wide, tall=tall),
        grid=(rows // tile,),
        in_specs=[
            row(width), row(width), *[row(mixture.shape[1]) for mixture in mixtures],
            *[ANYWHERE] * (len(wide.parts) + len(tall.parts)),
            whole(vecs.shape), whole((1, hidden_width)), whole(select.shape),
        ],
        out_specs=[
            row(width), row(hidden_width), row(hidden_width), row(width), row(width), row(width),
            row(width), row(width),
            pl.BlockSpec((PAIRS * ROW_GROUP, tile), lambda i: (0, i)),
            keep(4 * width), keep(hidden_width),
        ],
        out_shape=[
            shape((rows, width), BF), shape((rows, hidden_width), BF),
            shape((rows, hidden_width), BF), shape((rows, width), F32), shape((rows, width), BF),
            shape((rows, width), BF), shape((rows, width), BF), shape((rows, width), BF),
            shape((PAIRS * ROW_GROUP, rows), F32),
            shape((ROW_GROUP, 4 * width), F32), shape((ROW_GROUP, hidden_width), F32),
        ],
        scratch_shapes=[
            pltpu.VMEM(wide.shape, BF), pltpu.VMEM(tall.shape, BF),
            pltpu.SemaphoreType.DMA((wide.copies,)), pltpu.SemaphoreType.DMA((tall.copies,)),
        ],
        compiler_params=params(1),
        cost_estimate=cost(
            rows * width * (4 * width + 8 * hidden_width),
            rows * (width * 20 + hidden_width * 4) + 2 * width * (width + 2 * hidden_width),
            rows * hidden_width * 2,
        ),
        name="feed",
    )(x, g, *mixtures, *wide.arrays, *tall.arrays, vecs, be, select)


def lay_out(value, first_device, keep_ref, send_ref, rows, bits):
    chip = lax.axis_index("dp")
    core = lax.axis_index("blk")
    for index in range(value.shape[0] // rows):
        device = first_device + index
        slot = slot_of(lax.bitwise_xor(chip, device // 2), bits)
        block = value[index * rows : (index + 1) * rows].astype(keep_ref.dtype)

        @pl.when(core == index % 2)
        def _():
            keep_ref[slot] = block

        @pl.when(core != index % 2)
        def _():
            send_ref[slot] = block


def outer_tall_body(left_ref, right_ref, *outs, rows, bits):
    value = dot(left_ref[...], right_ref[...], TN)
    if bits is None:
        outs[0][...] = value.astype(outs[0].dtype)
    else:
        first = pl.program_id(0) * (value.shape[0] // rows)
        lay_out(value, first, outs[0], outs[1], rows, bits)


def outer_tall(left, right, rows, bits, dtype=BF):
    length, many = left.shape
    few = right.shape[1]
    chunk = 384
    if bits is None:
        out_specs = [pl.BlockSpec((chunk, few), lambda i: (i, 0))]
        out_shape = [jax.ShapeDtypeStruct((many, few), dtype)]
    else:
        shape = (many // (2 * rows), rows, few)
        out_specs = [pl.BlockSpec(shape, lambda i: (0, 0, 0))] * 2
        out_shape = [jax.ShapeDtypeStruct(shape, dtype)] * 2
    return pl.pallas_call(
        partial(outer_tall_body, rows=rows, bits=bits),
        grid=(many // chunk,),
        in_specs=[pl.BlockSpec((length, chunk), lambda i: (0, i)), whole((length, few))],
        out_specs=out_specs,
        out_shape=out_shape,
        compiler_params=params(1),
        cost_estimate=cost(2 * length * many * few, 2 * length * (many + few) + 2 * many * few),
        name="outer_tall",
    )(left, right)


def outer_wide_body(left_ref, *refs, pieces, rows, bits):
    right_refs = refs[:pieces]
    outs = refs[pieces:-1]
    turned = refs[-1]

    @pl.when(pl.program_id(0) == 0)
    def _():
        turned[...] = jnp.transpose(left_ref[...])

    if pieces == 1:
        right = right_refs[0][...]
    else:
        right = jnp.concatenate([ref[...] for ref in right_refs], axis=1)
    value = dot(turned[...], right)
    if bits is None:
        outs[0][...] = value.astype(outs[0].dtype)
    else:
        lay_out(value, 0, outs[0], outs[1], rows, bits)


def outer_wide(left, rights, rows, bits, dtype=BF):
    length, few = left.shape
    many = sum(right.shape[1] for right in rights)
    pieces = len(rights)
    chunk = 512 if pieces == 1 and many % 512 == 0 else many
    if bits is None:
        out_specs = [pl.BlockSpec((few, chunk), lambda i: (0, i))]
        out_shape = [jax.ShapeDtypeStruct((few, many), dtype)]
    else:
        slots = few // (2 * rows)
        out_specs = [pl.BlockSpec((slots, rows, chunk), lambda i: (0, 0, i))] * 2
        out_shape = [jax.ShapeDtypeStruct((slots, rows, many), dtype)] * 2
    return pl.pallas_call(
        partial(outer_wide_body, pieces=pieces, rows=rows, bits=bits),
        grid=(many // chunk,),
        in_specs=[whole((length, few))]
        + [
            pl.BlockSpec((length, chunk if pieces == 1 else right.shape[1]), lambda i: (0, i))
            for right in rights
        ],
        out_specs=out_specs,
        out_shape=out_shape,
        scratch_shapes=[pltpu.VMEM((few, length), BF)],
        compiler_params=params(1),
        cost_estimate=cost(2 * length * many * few, 2 * length * (many + few) + 2 * many * few),
        name="outer_wide",
    )(left, *rights)


def collect(grads, bits):
    if bits is None:
        return lax.psum_scatter(
            grads[0].astype(F32), ("dp", "blk"), scatter_dimension=0, tiled=True
        )
    held, sent = grads
    arrived = sibling(sent)
    for k in range(len(bits))[::-1]:
        half = 1 << k
        away = (held[half:].astype(F32) + arrived[half:].astype(F32)).astype(BF)
        held = (held[:half].astype(F32) + arrived[:half].astype(F32)).astype(BF)
        arrived = swap_bit(away, bits[k])
    return (held.astype(F32) + arrived.astype(F32))[0]


def collect_small(table):
    sizes = {"dp": lax.axis_size("dp"), "blk": lax.axis_size("blk")}
    if not quick_mesh(sizes):
        return lax.psum_scatter(table, ("dp", "blk"), scatter_dimension=0, tiled=True)[0]
    chip = lax.axis_index("dp")
    core = lax.axis_index("blk")
    held = table
    for bit in (3, 2, 1, 0):
        pairs = held.reshape(2, held.shape[0] // 2, held.shape[1])
        mine = (chip >> bit) & 1
        keep = jnp.where(mine == 0, pairs[0], pairs[1])
        away = jnp.where(mine == 0, pairs[1], pairs[0])
        held = keep + swap_bit(away, bit)
    keep = jnp.where(core == 0, held[0], held[1])
    away = jnp.where(core == 0, held[1], held[0])
    return keep + sibling(away)


def unproject_body(*refs, pieces):
    parts = [[ref[...] for ref in refs[pieces * k : pieces * (k + 1)]] for k in range(3)]
    w_ref, x_ref, vecs_ref, gm_ref, tg_ref, vec_ref = refs[3 * pieces :]
    width = x_ref.shape[1]

    @pl.when(pl.program_id(0) == 0)
    def _():
        vec_ref[...] = jnp.zeros_like(vec_ref)

    grads = [part[0] if pieces == 1 else jnp.concatenate(part, axis=1) for part in parts]
    u = dot(jnp.concatenate(grads, axis=1), w_ref[:, : 3 * width], NT)
    z, scale = normed(x_ref[...].astype(F32))
    back = norm_back(u, vecs_ref[0:1, :], z, scale)
    tg_ref[...] = (gm_ref[...] + back).astype(BF)
    vec_ref[:, :width] += fold_rows(u * z)
    vec_ref[:, width : 2 * width] += fold_rows(u)
    vec_ref[:, 2 * width : 3 * width] += fold_rows(grads[0].astype(F32))
    vec_ref[:, 3 * width :] += fold_rows(grads[2].astype(F32))


def unproject(dq, dk, dv, weight, x, vecs, gm):
    rows, width = x.shape
    tile = row_tile(rows)
    row = lambda cols: pl.BlockSpec((tile, cols), lambda i: (i, 0))
    grads = [*dq, *dk, *dv]
    return pl.pallas_call(
        partial(unproject_body, pieces=len(dq)),
        grid=(rows // tile,),
        in_specs=[row(grad.shape[1]) for grad in grads]
        + [whole(weight.shape), row(width), whole(vecs.shape), row(width)],
        out_specs=[row(width), pl.BlockSpec((ROW_GROUP, 4 * width), lambda i: (0, 0))],
        out_shape=[
            jax.ShapeDtypeStruct((rows, width), BF),
            jax.ShapeDtypeStruct((ROW_GROUP, 4 * width), F32),
        ],
        compiler_params=params(1),
        cost_estimate=cost(6 * rows * width * width, 2 * rows * width * 8 + 6 * width * width),
        name="unproject",
    )(*grads, weight, x, vecs, gm)


def pad_rows(values, rows):
    return jnp.pad(values, ((0, 0), (0, rows - values.shape[1]), (0, 0)))


def trade_clips(values):
    if lax.axis_size("blk") != 2:
        return lax.all_to_all(values, "blk", 0, 1, tiled=True)
    clips, rows, width = values.shape
    core = lax.axis_index("blk")
    pairs = values.reshape(2, clips // 2, rows, width)
    low, high = pairs[0], pairs[1]
    mine = jnp.where(core == 0, low, high)
    other = sibling(jnp.where(core == 0, high, low))
    return jnp.concatenate(
        [jnp.where(core == 0, mine, other), jnp.where(core == 0, other, mine)], axis=1
    )


def trade_back(values):
    if lax.axis_size("blk") != 2:
        return lax.all_to_all(values, "blk", 1, 0, tiled=True)
    clips, rows, width = values.shape
    core = lax.axis_index("blk")
    low, high = values[:, : rows // 2], values[:, rows // 2 :]
    mine = jnp.where(core == 0, low, high)
    other = sibling(jnp.where(core == 0, high, low))
    return jnp.concatenate(
        [jnp.where(core == 0, mine, other), jnp.where(core == 0, other, mine)], axis=0
    )


def key_mask(counts, cycle, rows_dev, rows_pad):
    position = jnp.arange(cycle * rows_pad, dtype=jnp.int32)
    block = position // rows_pad
    offset = position % rows_pad
    column = block * ((rows_dev - 2) // FREQ) + (offset - 2) // FREQ
    seen = jnp.where(
        (offset < 2)[None, :], (block == 0)[None, :], column[None, :] < counts[:, None]
    ) & (offset < rows_dev)[None, :]
    lane = jnp.arange(LANES, dtype=jnp.int32)
    return jnp.where(seen[:, :, None] | (lane > 0)[None, None, :], 0.0, NEGATIVE).astype(BF)


GROUPS = ((0, 2), (2, 2), (4, 2))


def local(
    tokens, counts, attend_gain, attend_shift, merged_weight, query_bias, value_bias,
    output_weight, output_bias, feed_gain, feed_shift, expand_weight, expand_bias,
    shrink_weight, shrink_bias, cotangent,
):
    clips, rows_dev, width = tokens.shape
    chips, cycle = lax.axis_size("dp"), lax.axis_size("blk")
    quick = quick_mesh({"dp": chips, "blk": cycle})
    rows_pad = -(-rows_dev // 16) * 16
    traded = clips % cycle == 0
    weight_rows = merged_weight.shape[0]
    tall_rows = shrink_weight.shape[0]
    hidden_width = expand_weight.shape[1]

    bias_cols = expand_bias.reshape(weight_rows, -1)
    vec_cols = jnp.stack(
        [
            attend_gain, attend_shift, query_bias, value_bias,
            output_bias, feed_gain, feed_shift, shrink_bias,
        ],
        axis=1,
    )
    extra = jnp.concatenate([vec_cols, bias_cols], axis=1)
    extra = jnp.pad(extra, ((0, 0), (0, VEC_COLS - extra.shape[1])))
    first_pack = jnp.concatenate([merged_weight, extra], axis=1)
    wide_pack = jnp.concatenate([expand_weight, output_weight], axis=1)
    if quick:
        cut = first_pack.shape[1] // 4
        merged_full = gather_halves(first_pack, ((cut, BITS_FIRST), (cut, BITS_SECOND)))
        wide = gather_halves(wide_pack, ((wide_pack.shape[1] // 2, BITS_FIRST),))
        tall = gather_rows(shrink_weight, BITS_SECOND)
    else:
        merged_full = gather_plain(first_pack)
        wide = gather_plain(wide_pack)
        tall = gather_plain(shrink_weight)

    x = pad_rows(tokens, rows_pad)
    g = pad_rows(cotangent, rows_pad)
    if traded:
        x = trade_clips(x)
        g = trade_clips(g)
        held = clips // cycle
        own_counts = lax.dynamic_slice_in_dim(counts, lax.axis_index("blk") * held, held)
    else:
        held = clips
        own_counts = counts
    queries = x.shape[1]
    total = held * queries
    x = x.reshape(total, width)
    g = g.reshape(total, width)
    mask = key_mask(own_counts, cycle, rows_dev, rows_pad)

    attend_input, merged, weight_flat, vecs = project(x, merged_full)
    bias_row = vecs[8 : 8 + bias_cols.shape[1]].T.reshape(1, hidden_width)
    merged = merged.reshape(held, queries, 3 * width)
    if traded:
        keys, key_base = merged, PAIRS
    else:
        keys = lax.all_gather(merged[:, :, width:], "blk", axis=1, tiled=True)
        key_base = 0
    mixtures, sums = [], []
    for first, count in GROUPS:
        mixture, log_total = attend(merged, keys, key_base, mask, first, count)
        mixtures.append(mixture.reshape(total, count * LANES))
        sums.append(log_total)
    (
        result, hidden, grad_preact, grad_middle, attended, grad_branch, feed_input, grad_attended,
        delta, feed_vec, expand_vec,
    ) = feed(x, g, mixtures, wide, tall, vecs, bias_row)

    first_bits, second_bits = (BITS_FIRST, BITS_SECOND) if quick else (None, None)
    shrink_grad = collect(outer_tall(hidden, g, tall_rows, second_bits), second_bits)
    expand_grad = collect(outer_wide(feed_input, [grad_preact], weight_rows, first_bits), first_bits)
    output_grad = collect(outer_wide(attended, [grad_branch], weight_rows, second_bits), second_bits)
    delta = delta.reshape(PAIRS * ROW_GROUP, held, queries).transpose(1, 0, 2)
    grad_heads = grad_attended.reshape(held, queries, width)
    dq, dk, dv = [], [], []
    for (first, count), log_total in zip(GROUPS, sums):
        parts = attend_back(merged, keys, key_base, grad_heads, mask, log_total, delta, first, count)
        if not traded:
            parts = (
                parts[0],
                lax.psum_scatter(parts[1], "blk", scatter_dimension=1, tiled=True),
                lax.psum_scatter(parts[2], "blk", scatter_dimension=1, tiled=True),
            )
        for into, part in zip((dq, dk, dv), parts):
            into.append(part.reshape(total, count * LANES))
    query_grad = collect(outer_wide(attend_input, dq, weight_rows, first_bits), first_bits)
    key_grad = collect(outer_wide(attend_input, dk, weight_rows, second_bits), second_bits)
    value_grad = collect(outer_wide(attend_input, dv, weight_rows, first_bits), first_bits)
    tokens_grad, attend_vec = unproject(dq, dk, dv, weight_flat, x, vecs, grad_middle)

    devices = chips * cycle
    rows_of = lambda values: jnp.sum(values, axis=0).reshape(-1, devices, weight_rows)
    small = jnp.concatenate([rows_of(attend_vec), rows_of(feed_vec)], axis=0)
    small = small.transpose(1, 0, 2).reshape(devices, 8 * weight_rows)
    small = jnp.concatenate([small, jnp.sum(expand_vec, axis=0).reshape(devices, -1)], axis=1)
    small = collect_small(small)
    vec = lambda k: small[k * weight_rows : (k + 1) * weight_rows]

    def home(values):
        values = values.reshape(held, queries, width)
        if traded:
            values = trade_back(values)
        return values[:, :rows_dev]

    return (
        home(result),
        home(tokens_grad),
        vec(0),
        vec(1),
        jnp.concatenate([query_grad, key_grad, value_grad], axis=1),
        vec(2),
        vec(3),
        output_grad,
        vec(6),
        vec(4),
        vec(5),
        expand_grad,
        small[8 * weight_rows :],
        shrink_grad,
        vec(7),
    )


def solution(mesh):
    rows = P("dp", "blk", None)
    vector = P(("dp", "blk"))
    matrix = P(("dp", "blk"), None)
    in_specs = (
        rows, P("dp"), vector, vector, matrix, vector, vector, matrix, vector, vector, vector,
        matrix, vector, matrix, vector, rows,
    )
    out_specs = (
        rows, rows, vector, vector, matrix, vector, vector, matrix, vector, vector, vector,
        matrix, vector, matrix, vector,
    )
    return jax.shard_map(local, mesh=mesh, in_specs=in_specs, out_specs=out_specs, check_vma=False)
```

time: 914 us -> 493 us (0.54)
  matrix products: 400 us -> 0 us
  Pallas kernels: 0 us -> 233 us
  local copies, waits for them, and re-layouts: 140 us -> 33.3 us
  blocking collectives: 86.6 us -> 0 us
  waiting for transfers between devices: 192 us -> 128 us
  starting transfers between devices: 2.2 us -> 63.8 us
  other arithmetic: 66.2 us -> 25.9 us
  between operations: 15.5 us -> 1.64 us
    dot_general x28 -> x0, matrix products: 400 us -> none  [the longest x6 51.7 us: times_transposed(): lax.dot_general(left_side, right_side, (((1,), (1,)), ((), ())), preferre...]
    pallas_call x0 -> x15, Pallas kernels: none -> 233 us  [the longest x3 61.2 us: attend_back(): pl.pallas_call(partial(attend_back_body, tile=tile), grid=(clips, count),...]
    ppermute x6 -> x61, waiting for transfers between devices: 0.02 us -> 128 us  [the longest x44 127 us: swap_bit(): lax.ppermute(block, 'dp', [(i, i ^ 1 << bit) for i in range(lax.axis_size...]
    unnamed x11 -> x0, waiting for transfers between devices: 128 us -> none
    unnamed x2 -> x0, blocking collectives: 86.6 us -> none
    ppermute x6 -> x61, starting transfers between devices: 1.55 us -> 63.8 us  [the longest x44 59.3 us: swap_bit(): lax.ppermute(block, 'dp', [(i, i ^ 1 << bit) for i in range(lax.axis_size...]
    reduce_sum x10 -> x3, other arithmetic: 49.7 us -> 0.98 us  [the longest x2 0.95 us: local(): jnp.sum(values, axis=0).reshape(-1, devices, weight_rows)]
    convert_element_type x15 -> x0, local copies, waits for them, and re-layouts: 47.3 us -> none  [the longest x2 7.97 us: local(): inputs = tokens.reshape(total_rows, width).astype(jnp.float32)]
  transfers between devices with their start and end apart: 16 -> 61, of which waited for: 4 -> 28; matrix products, arithmetic and copies ran while one was open for 58% -> 11% of each run, Pallas kernels for 0% -> 34%
where the time goes in v1:
time: 493 us; the launch traced here: 485 us
  Pallas kernels  233 us (47%)
  waiting for transfers between devices  128 us (26%)
  starting transfers between devices  63.8 us (13%)
  local copies, waits for them, and re-layouts  33.3 us (7%)
  other arithmetic  25.9 us (5%)
    ppermute x44, waiting for transfers between devices, swap_bit(): lax.ppermute(block, 'dp', [(i, i ^ 1 << bit) for i in range(lax.axis_size...  127 us
    pallas_call x3, Pallas kernels, attend_back(): pl.pallas_call(partial(attend_back_body, tile=tile), grid=(clips, count),...  61.2 us
    ppermute x44, starting transfers between devices, swap_bit(): lax.ppermute(block, 'dp', [(i, i ^ 1 << bit) for i in range(lax.axis_size...  59.3 us
    pallas_call x1, Pallas kernels, feed(): pl.pallas_call(partial(feed_body, chunk=512, mixes=len(mixtures), wide=wi...  50.5 us
    pallas_call x3, Pallas kernels, attend(): pl.pallas_call(partial(attend_body, tile=tile), grid=(clips, count), in_s...  50 us
    pallas_call x5, Pallas kernels, outer_wide(): pl.pallas_call(partial(outer_wide_body, pieces=pieces, rows=rows, bits=bi...  33.9 us
    unnamed x57, local copies, waits for them, and re-layouts  18.6 us
    pallas_call x1, Pallas kernels, outer_tall(): pl.pallas_call(partial(outer_tall_body, rows=rows, bits=bits), grid=(many...  13.1 us
  transfers between devices with their start and end apart: 61, of which 28 were waited for; matrix products, arithmetic and copies ran while one was open for 11% of the time, Pallas kernels for 34%

profile of v1, /device:TPU:0, one launch (start us, length us, event | category | flops | bytes accessed | tf_op | source)
XLA Modules:
  0.0 485.3 jit_solution(8839295063505366250)
XLA Ops:
  38.5 5.7 %collective-permute-done.9 = bf16[2,48,640]{2,1,0:T(8,128)(2,1)S(1)} collective-permute-done((bf16[2,48,640]{2,1,0:T(8,128)(2,1)S(1)}, bf16[2,48,640]{2,1,0:T(8,128)(2,1)S(1)}, u32[]{:S(2)}, u32[]{:S(2)}) %collective-permute-start.9) | collective-permute-done | bytes 122912 | tf_op jit(solution)/shard_map/ppermute | solution.py:82
  64.8 14.0 %collective-permute-done.16 = bf16[4,48,1920]{2,1,0:T(8,128)(2,1)S(1)} collective-permute-done((bf16[4,48,1920]{2,1,0:T(8,128)(2,1)S(1)}, bf16[4,48,1920]{2,1,0:T(8,128)(2,1)S(1)}, u32[]{:S(2)}, u32[]{:S(2)}) %collective-permute-start.16) | collective-permute-done | bytes 737312 | tf_op jit(solution)/shard_map/ppermute | solution.py:82
  80.5 6.2 %collective-permute-done.11 = bf16[8,48,640]{2,1,0:T(8,128)(2,1)S(1)} collective-permute-done((bf16[8,48,640]{2,1,0:T(8,128)(2,1)S(1)}, bf16[8,48,640]{2,1,0:T(8,128)(2,1)S(1)}, u32[]{:S(2)}, u32[]{:S(2)}) %collective-permute-start.11) | collective-permute-done | bytes 491552 | tf_op jit(solution)/shard_map/ppermute | solution.py:82
  96.3 24.3 %collective-permute-done.17 = bf16[8,48,1920]{2,1,0:T(8,128)(2,1)S(1)} collective-permute-done((bf16[8,48,1920]{2,1,0:T(8,128)(2,1)S(1)}, bf16[8,48,1920]{2,1,0:T(8,128)(2,1)S(1)}, u32[]{:S(2)}, u32[]{:S(2)}) %collective-permute-start.17) | collective-permute-done | bytes 1474592 | tf_op jit(solution)/shard_map/ppermute | solution.py:82
  126.6 12.2 %project.1 = (bf16[1280,768]{1,0:T(8,128)(2,1)}, bf16[1280,2304]{1,0:T(8,128)(2,1)}, bf16[768,2560]{1,0:T(8,128)(2,1)}, f32[16,768]{1,0:T(8,128)}) custom-call(bf16[1280,768]{1,0:T(8,128)(2,1)} %maximum_bitcast_fusion.refs_0_.refs_10_, bf16[16,48,640]{2,1,0:T(8,128)(2,1)} %copy-done.13, bf16[16,48,640]{2,1,0:T(8,128)(2,1)} %collective-permute-done.7.refs_2_, ...), custom_call_target="tpu_custom_call" | custom-call | flops 4529848320 | bytes 13369344 | tf_op jit(solution)/shard_map/project/pallas_call | solution.py:231
  140.6 16.5 %attend.4 = (f32[1,1280,256]{2,1,0:T(8,128)}, f32[1,16,1280]{2,1,0:T(8,128)}) custom-call(bf16[1,1280,2304]{2,1,0:T(8,128)(2,1)} %bitcast.76, bf16[1,1280,2304]{2,1,0:T(8,128)(2,1)} %bitcast.77, bf16[1,1280,2304]{2,1,0:T(8,128)(2,1)} %bitcast.78, bf16[1,1280,128]{2,1,0:T(8,128)(2,1)} %select_convert_fusion.mask_ref), custom_call_target="tpu_custom_call" | custom-call | flops 6710886400 | bytes 3276800 | tf_op jit(solution)/shard_map/attend/pallas_call | solution.py:293
  157.1 17.0 %attend.5 = (f32[1,1280,256]{2,1,0:T(8,128)}, f32[1,16,1280]{2,1,0:T(8,128)}) custom-call(bf16[1,1280,2304]{2,1,0:T(8,128)(2,1)} %bitcast.79, bf16[1,1280,2304]{2,1,0:T(8,128)(2,1)} %bitcast.80, bf16[1,1280,2304]{2,1,0:T(8,128)(2,1)} %bitcast.81, bf16[1,1280,128]{2,1,0:T(8,128)(2,1)} %select_convert_fusion.mask_ref), custom_call_target="tpu_custom_call" | custom-call | flops 6710886400 | bytes 3276800 | tf_op jit(solution)/shard_map/attend/pallas_call | solution.py:293
  174.1 16.5 %attend.3 = (f32[1,1280,256]{2,1,0:T(8,128)}, f32[1,16,1280]{2,1,0:T(8,128)}) custom-call(bf16[1,1280,2304]{2,1,0:T(8,128)(2,1)} %bitcast.82, bf16[1,1280,2304]{2,1,0:T(8,128)(2,1)} %bitcast.83, bf16[1,1280,2304]{2,1,0:T(8,128)(2,1)} %bitcast.84, bf16[1,1280,128]{2,1,0:T(8,128)(2,1)} %select_convert_fusion.mask_ref), custom_call_target="tpu_custom_call" | custom-call | flops 6710886400 | bytes 3276800 | tf_op jit(solution)/shard_map/attend/pallas_call | solution.py:293
  192.0 50.5 %feed.1 = (bf16[1280,768]{1,0:T(8,128)(2,1)}, bf16[1280,3072]{1,0:T(8,128)(2,1)}, bf16[1280,3072]{1,0:T(8,128)(2,1)}, f32[1280,768]{1,0:T(8,128)}, bf16[1280,768...) custom-call(bf16[1280,768]{1,0:T(8,128)(2,1)} %maximum_bitcast_fusio, ...), custom_call_target="tpu_custom_call" | custom-call | flops 27179089920 | bytes 46006272 | tf_op jit(solution)/shard_map/feed/pallas_call | solution.py:494
  242.5 13.1 %outer_tall.1 = (bf16[16,96,768]{2,1,0:T(8,128)(2,1)}, bf16[16,96,768]{2,1,0:T(8,128)(2,1)}) custom-call(bf16[1280,3072]{1,0:T(8,128)(2,1)} %get-tuple-element.100.left_ref, bf16[1280,768]{1,0:T(8,128)(2,1)} %maximum_bitcast_fusion.1.refs_1_.right_ref), custom_call_target="tpu_custom_call" | custom-call | flops 6039797760 | bytes 14548992 | tf_op jit(solution)/shard_map/outer_tall/pallas_call | solution.py:566
  255.5 5.2 %outer_wide.8 = (bf16[16,24,768]{2,1,0:T(8,128)(2,1)}, bf16[16,24,768]{2,1,0:T(8,128)(2,1)}) custom-call(bf16[1280,768]{1,0:T(8,128)(2,1)} %get-tuple-element.92.left_ref, bf16[1280,768]{1,0:T(8,128)(2,1)} %get-tuple-element.93.refs_0_), custom_call_target="tpu_custom_call" | custom-call | flops 1509949440 | bytes 5111808 | tf_op jit(solution)/shard_map/outer_wide/pallas_call | solution.py:610
  260.8 20.3 %attend_back.5 = (bf16[1,1280,256]{2,1,0:T(8,128)(2,1)}, bf16[1,1280,256]{2,1,0:T(8,128)(2,1)}, bf16[1,1280,256]{2,1,0:T(8,128)(2,1)}) custom-call(bf16[1,1280,2304]{2,1,0:T(8,128)(2,1)} %bitcast.85, bf16[1,1280,2304]{2,1,0:T(8,128)(2,1)} %bitcast.86, bf16[1,1280,2304]{2,1,0:T(8,128)(2,1)} %bitcast.87, bf16[1,1280,768]{2,1,0:T(8,128)(2,1)} %bitcast.94, ...), custom_call_target="tpu_custom_call" | custom-call | flops 15099494400 | bytes 4587520 | tf_op jit(solution)/shard_map/attend_back/pallas_call | solution.py:367
  281.1 20.5 %attend_back.4 = (bf16[1,1280,256]{2,1,0:T(8,128)(2,1)}, bf16[1,1280,256]{2,1,0:T(8,128)(2,1)}, bf16[1,1280,256]{2,1,0:T(8,128)(2,1)}) custom-call(bf16[1,1280,2304]{2,1,0:T(8,128)(2,1)} %bitcast.88, bf16[1,1280,2304]{2,1,0:T(8,128)(2,1)} %bitcast.89, bf16[1,1280,2304]{2,1,0:T(8,128)(2,1)} %bitcast.90, bf16[1,1280,768]{2,1,0:T(8,128)(2,1)} %bitcast.95, ...), custom_call_target="tpu_custom_call" | custom-call | flops 15099494400 | bytes 4587520 | tf_op jit(solution)/shard_map/attend_back/pallas_call | solution.py:367
  301.6 20.4 %attend_back.3 = (bf16[1,1280,256]{2,1,0:T(8,128)(2,1)}, bf16[1,1280,256]{2,1,0:T(8,128)(2,1)}, bf16[1,1280,256]{2,1,0:T(8,128)(2,1)}) custom-call(bf16[1,1280,2304]{2,1,0:T(8,128)(2,1)} %bitcast.91, bf16[1,1280,2304]{2,1,0:T(8,128)(2,1)} %bitcast.92, bf16[1,1280,2304]{2,1,0:T(8,128)(2,1)} %bitcast.93, bf16[1,1280,768]{2,1,0:T(8,128)(2,1)} %bitcast.96, ...), custom_call_target="tpu_custom_call" | custom-call | flops 15099494400 | bytes 4587520 | tf_op jit(solution)/shard_map/attend_back/pallas_call | solution.py:367
  321.9 5.2 %outer_wide.5 = (bf16[16,24,768]{2,1,0:T(8,128)(2,1)}, bf16[16,24,768]{2,1,0:T(8,128)(2,1)}) custom-call(bf16[1280,768]{1,0:T(8,128)(2,1)} %get-tuple-element.85.left_ref, bf16[1280,256]{1,0:T(8,128)(2,1)} %bitcast.116, bf16[1280,256]{1,0:T(8,128)(2,1)} %bitcast.114, bf16[1280,256]{1,0:T(8,128)(2,1)} %bitcast.112), custom_call_target="tpu_custom_call" | custom-call | flops 1509949440 | bytes 5111808 | tf_op jit(solution)/shard_map/outer_wide/pallas_call | solution.py:610
  327.6 12.2 %unproject.1 = (bf16[1280,768]{1,0:T(8,128)(2,1)}, f32[8,3072]{1,0:T(8,128)}) custom-call(bf16[1280,256]{1,0:T(8,128)(2,1)} %bitcast.117, bf16[1280,256]{1,0:T(8,128)(2,1)} %bitcast.115, bf16[1280,256]{1,0:T(8,128)(2,1)} %bitcast.113, bf16[1280,256]{1,0:T(8,128)(2,1)} %bitcast.110, bf16[1280,256]{1,0:T(8,128)(2,1)} %bitcast.108, ...), custom_call_target="tpu_custom_call" | custom-call | flops 4529848320 | bytes 19267584 | tf_op jit(solution)/shard_map/unproject/pallas_call | solution.py:685
  344.5 12.8 %outer_wide.9 = (bf16[16,24,3072]{2,1,0:T(8,128)(2,1)}, bf16[16,24,3072]{2,1,0:T(8,128)(2,1)}) custom-call(bf16[1280,768]{1,0:T(8,128)(2,1)} %get-tuple-element.96.left_ref, bf16[1280,3072]{1,0:T(8,128)(2,1)} %get-tuple-element.97.refs_0_), custom_call_target="tpu_custom_call" | custom-call | flops 6039797760 | bytes 14548992 | tf_op jit(solution)/shard_map/outer_wide/pallas_call | solution.py:610
  366.6 5.2 %outer_wide.6 = (bf16[16,24,768]{2,1,0:T(8,128)(2,1)}, bf16[16,24,768]{2,1,0:T(8,128)(2,1)}) custom-call(bf16[1280,768]{1,0:T(8,128)(2,1)} %get-tuple-element.85.left_ref, bf16[1280,256]{1,0:T(8,128)(2,1)} %bitcast.111, bf16[1280,256]{1,0:T(8,128)(2,1)} %bitcast.109, bf16[1280,256]{1,0:T(8,128)(2,1)} %bitcast.107), custom_call_target="tpu_custom_call" | custom-call | flops 1509949440 | bytes 5111808 | tf_op jit(solution)/shard_map/outer_wide/pallas_call | solution.py:610
  371.9 5.5 %outer_wide.7 = (bf16[16,24,768]{2,1,0:T(8,128)(2,1)}, bf16[16,24,768]{2,1,0:T(8,128)(2,1)}) custom-call(bf16[1280,768]{1,0:T(8,128)(2,1)} %get-tuple-element.85.left_ref, bf16[1280,256]{1,0:T(8,128)(2,1)} %bitcast.105, bf16[1280,256]{1,0:T(8,128)(2,1)} %bitcast.103, bf16[1280,256]{1,0:T(8,128)(2,1)} %bitcast.101), custom_call_target="tpu_custom_call" | custom-call | flops 1509949440 | bytes 5111808 | tf_op jit(solution)/shard_map/outer_wide/pallas_call | solution.py:610
  385.6 6.8 %collective-permute-done.47 = bf16[8,24,768]{2,1,0:T(8,128)(2,1)S(1)} collective-permute-done((bf16[8,24,768]{2,1,0:T(8,128)(2,1)S(1)}, bf16[8,24,768]{2,1,0:T(8,128)(2,1)S(1)}, u32[]{:S(2)}, u32[]{:S(2)}) %collective-permute-start.47) | collective-permute-done | bytes 294944 | tf_op jit(solution)/shard_map/ppermute | solution.py:82
  394.8 6.0 %collective-permute-done.37 = bf16[8,24,768]{2,1,0:T(8,128)(2,1)S(1)} collective-permute-done((bf16[8,24,768]{2,1,0:T(8,128)(2,1)S(1)}, bf16[8,24,768]{2,1,0:T(8,128)(2,1)S(1)}, u32[]{:S(2)}, u32[]{:S(2)}) %collective-permute-start.37) | collective-permute-done | bytes 294944 | tf_op jit(solution)/shard_map/ppermute | solution.py:82
  433.0 15.7 %collective-permute-done.57 = bf16[8,96,768]{2,1,0:T(8,128)(2,1)S(1)} collective-permute-done((bf16[8,96,768]{2,1,0:T(8,128)(2,1)S(1)}, bf16[8,96,768]{2,1,0:T(8,128)(2,1)S(1)}, u32[]{:S(2)}, u32[]{:S(2)}) %collective-permute-start.57) | collective-permute-done | bytes 1179680 | tf_op jit(solution)/shard_map/ppermute | solution.py:82
  456.1 7.3 %collective-permute-done.58 = bf16[4,96,768]{2,1,0:T(8,128)(2,1)S(1)} collective-permute-done((bf16[4,96,768]{2,1,0:T(8,128)(2,1)S(1)}, bf16[4,96,768]{2,1,0:T(8,128)(2,1)S(1)}, u32[]{:S(2)}, u32[]{:S(2)}) %collective-permute-start.58) | collective-permute-done | bytes 589856 | tf_op jit(solution)/shard_map/ppermute | solution.py:82
  468.3 5.8 %collective-permute-done.59 = bf16[2,96,768]{2,1,0:T(8,128)(2,1)S(1)} collective-permute-done((bf16[2,96,768]{2,1,0:T(8,128)(2,1)S(1)}, bf16[2,96,768]{2,1,0:T(8,128)(2,1)S(1)}, u32[]{:S(2)}, u32[]{:S(2)}) %collective-permute-start.59) | collective-permute-done | bytes 294944 | tf_op jit(solution)/shard_map/ppermute | solution.py:82
  (278 shorter events, 158.9 us)
Async XLA Ops:
  3.0 23.6 %collective-permute-start.13 = (bf16[24,1920]{1,0:T(8,128)(2,1)}, bf16[24,1920]{1,0:T(8,128)(2,1)S(1)}, u32[]{:S(2)}, u32[]{:S(2)}) collective-permute-start(bf16[24,1920]{1,0:T(8,128)(2,1)} %get-tuple-element.181), channel_id=1, source_target_pairs={{0,1},{1,0},{2,3},{3,2},{4,5},{5,4},{6,7},{7,6},{8,9},{9,8},{10,11... | collective-permute-start | bytes 276488 | tf_op jit(solution)/shard_map/ppermute | solution.py:86
  14.3 74.2 %collective-permute-start = (bf16[1,640,768]{2,1,0:T(8,128)(2,1)}, bf16[1,640,768]{2,1,0:T(8,128)(2,1)S(1)}, u32[]{:S(2)}, u32[]{:S(2)}) collective-permute-start(bf16[1,640,768]{2,1,0:T(8,128)(2,1)} %broadcast_select_fusion.14), channel_id=1, source_target_pairs={{0,1},{1,0},{2,3},{3,2},{4,5},{5,4},{6,7},{7,6},{8,9},{9,8},{10,11... | collective-permute-start | bytes 2949128 | tf_op jit(solution)/shard_map/ppermute | solution.py:86
  14.8 21.3 %collective-permute-start.19 = (bf16[1,96,768]{2,1,0:T(8,128)(2,1)S(1)}, bf16[1,96,768]{2,1,0:T(8,128)(2,1)S(1)}, u32[]{:S(2)}, u32[]{:S(2)}) collective-permute-start(bf16[1,96,768]{2,1,0:T(8,128)(2,1)S(1)} %bitcast.63), channel_id=1, source_target_pairs={{0,16},{2,18},{4,20},{6,22},{8,24},{10,26},{12,28},{14,30},{16,0},... | collective-permute-start | bytes 442376 | tf_op jit(solution)/shard_map/ppermute | solution.py:82
  21.1 68.5 %collective-permute-start.1 = (bf16[1,640,768]{2,1,0:T(8,128)(2,1)}, bf16[1,640,768]{2,1,0:T(8,128)(2,1)}, u32[]{:S(2)}, u32[]{:S(2)}) collective-permute-start(bf16[1,640,768]{2,1,0:T(8,128)(2,1)} %broadcast_select_fusion.10), channel_id=1, source_target_pairs={{0,1},{1,0},{2,3},{3,2},{4,5},{5,4},{6,7},{7,6},{8,9},{9,8},{10,11... | collective-permute-start | bytes 2949128 | tf_op jit(solution)/shard_map/ppermute | solution.py:86
  46.9 14.7 %collective-permute-start.10 = (bf16[4,48,640]{2,1,0:T(8,128)(2,1)S(1)}, bf16[4,48,640]{2,1,0:T(8,128)(2,1)S(1)}, u32[]{:S(2)}, u32[]{:S(2)}) collective-permute-start(bf16[4,48,640]{2,1,0:T(8,128)(2,1)S(1)} %pad_maximum_fusion.11), channel_id=1, source_target_pairs={{0,4},{2,6},{4,0},{6,2},{8,12},{10,14},{12,8},{14,10},{16,20},{18,... | collective-permute-start | bytes 737288 | tf_op jit(solution)/shard_map/ppermute | solution.py:82
  59.3 19.5 %collective-permute-start.16 = (bf16[4,48,1920]{2,1,0:T(8,128)(2,1)S(1)}, bf16[4,48,1920]{2,1,0:T(8,128)(2,1)S(1)}, u32[]{:S(2)}, u32[]{:S(2)}) collective-permute-start(bf16[4,48,1920]{2,1,0:T(8,128)(2,1)S(1)} %pad_maximum_fusion.4), channel_id=1, source_target_pairs={{0,2},{2,0},{4,6},{6,4},{8,10},{10,8},{12,14},{14,12},{16,18},{18,... | collective-permute-start | bytes 2211848 | tf_op jit(solution)/shard_map/ppermute | solution.py:82
  61.7 25.0 %collective-permute-start.11 = (bf16[8,48,640]{2,1,0:T(8,128)(2,1)S(1)}, bf16[8,48,640]{2,1,0:T(8,128)(2,1)S(1)}, u32[]{:S(2)}, u32[]{:S(2)}) collective-permute-start(bf16[8,48,640]{2,1,0:T(8,128)(2,1)S(1)} %pad_maximum_fusion.7), channel_id=1, source_target_pairs={{0,2},{2,0},{4,6},{6,4},{8,10},{10,8},{12,14},{14,12},{16,18},{18,... | collective-permute-start | bytes 1474568 | tf_op jit(solution)/shard_map/ppermute | solution.py:82
  62.4 26.0 %collective-permute-start.6 = (bf16[8,48,640]{2,1,0:T(8,128)(2,1)S(1)}, bf16[8,48,640]{2,1,0:T(8,128)(2,1)S(1)}, u32[]{:S(2)}, u32[]{:S(2)}) collective-permute-start(bf16[8,48,640]{2,1,0:T(8,128)(2,1)S(1)} %pad_maximum_fusion.6), channel_id=1, source_target_pairs={{0,4},{2,6},{4,0},{6,2},{8,12},{10,14},{12,8},{14,10},{16,20},{18,... | collective-permute-start | bytes 1474568 | tf_op jit(solution)/shard_map/ppermute | solution.py:82
  86.7 33.8 %collective-permute-start.17 = (bf16[8,48,1920]{2,1,0:T(8,128)(2,1)S(1)}, bf16[8,48,1920]{2,1,0:T(8,128)(2,1)S(1)}, u32[]{:S(2)}, u32[]{:S(2)}) collective-permute-start(bf16[8,48,1920]{2,1,0:T(8,128)(2,1)S(1)} %pad_maximum_fusion.2), channel_id=1, source_target_pairs={{0,4},{2,6},{4,0},{6,2},{8,12},{10,14},{12,8},{14,10},{16,20},{18,... | collective-permute-start | bytes 4423688 | tf_op jit(solution)/shard_map/ppermute | solution.py:82
  88.3 37.3 %collective-permute-start.12 = (bf16[16,48,640]{2,1,0:T(8,128)(2,1)S(1)}, bf16[16,48,640]{2,1,0:T(8,128)(2,1)S(1)}, u32[]{:S(2)}, u32[]{:S(2)}) collective-permute-start(bf16[16,48,640]{2,1,0:T(8,128)(2,1)S(1)} %constant_dynamic-update-slice_fusion.5.refs_3_), channel_id=1, source_target_pairs={{0,1},{1,0},{2,3},{3,2},{4,5},{5,4},{6,7},{7,6},{8,9},{9,8},{10,11... | collective-permute-start | bytes 2949128 | tf_op jit(solution)/shard_map/ppermute | solution.py:86
  88.5 38.1 %collective-permute-start.7 = (bf16[16,48,640]{2,1,0:T(8,128)(2,1)S(1)}, bf16[16,48,640]{2,1,0:T(8,128)(2,1)}, u32[]{:S(2)}, u32[]{:S(2)}) collective-permute-start(bf16[16,48,640]{2,1,0:T(8,128)(2,1)S(1)} %constant_dynamic-update-slice_fusion.refs_1_), channel_id=1, source_target_pairs={{0,1},{1,0},{2,3},{3,2},{4,5},{5,4},{6,7},{7,6},{8,9},{9,8},{10,11... | collective-permute-start | bytes 2949128 | tf_op jit(solution)/shard_map/ppermute | solution.py:86
  92.4 31.7 %collective-permute-start.22 = (bf16[8,96,768]{2,1,0:T(8,128)(2,1)S(1)}, bf16[8,96,768]{2,1,0:T(8,128)(2,1)S(1)}, u32[]{:S(2)}, u32[]{:S(2)}) collective-permute-start(bf16[8,96,768]{2,1,0:T(8,128)(2,1)S(1)} %pad_maximum_fusion.3), channel_id=1, source_target_pairs={{0,2},{2,0},{4,6},{6,4},{8,10},{10,8},{12,14},{14,12},{16,18},{18,... | collective-permute-start | bytes 3538952 | tf_op jit(solution)/shard_map/ppermute | solution.py:82
  121.7 68.9 %collective-permute-start.18 = (bf16[16,48,1920]{2,1,0:T(8,128)(2,1)}, bf16[16,48,1920]{2,1,0:T(8,128)(2,1)}, u32[]{:S(2)}, u32[]{:S(2)}) collective-permute-start(bf16[16,48,1920]{2,1,0:T(8,128)(2,1)} %constant_dynamic-update-slice_fusion.12.refs_5_), channel_id=1, source_target_pairs={{0,1},{1,0},{2,3},{3,2},{4,5},{5,4},{6,7},{7,6},{8,9},{9,8},{10,11... | collective-permute-start | bytes 8847368 | tf_op jit(solution)/shard_map/ppermute | solution.py:86
  125.1 65.5 %collective-permute-start.23 = (bf16[16,96,768]{2,1,0:T(8,128)(2,1)}, bf16[16,96,768]{2,1,0:T(8,128)(2,1)S(1)}, u32[]{:S(2)}, u32[]{:S(2)}) collective-permute-start(bf16[16,96,768]{2,1,0:T(8,128)(2,1)} %constant_dynamic-update-slice_fusion.17.refs_7_), channel_id=1, source_target_pairs={{0,1},{1,0},{2,3},{3,2},{4,5},{5,4},{6,7},{7,6},{8,9},{9,8},{10,11... | collective-permute-start | bytes 7077896 | tf_op jit(solution)/shard_map/ppermute | solution.py:86
  260.8 118.8 %collective-permute-start.46 = (bf16[16,24,768]{2,1,0:T(8,128)(2,1)}, bf16[16,24,768]{2,1,0:T(8,128)(2,1)}, u32[]{:S(2)}, u32[]{:S(2)}) collective-permute-start(bf16[16,24,768]{2,1,0:T(8,128)(2,1)} %get-tuple-element.95), channel_id=1, source_target_pairs={{0,1},{1,0},{2,3},{3,2},{4,5},{5,4},{6,7},{7,6},{8,9},{9,8},{10,11... | collective-permute-start | bytes 1769480 | tf_op jit(solution)/shard_map/ppermute | solution.py:86
  327.1 53.9 %collective-permute-start.31 = (bf16[16,24,768]{2,1,0:T(8,128)(2,1)}, bf16[16,24,768]{2,1,0:T(8,128)(2,1)}, u32[]{:S(2)}, u32[]{:S(2)}) collective-permute-start(bf16[16,24,768]{2,1,0:T(8,128)(2,1)} %get-tuple-element.87), channel_id=1, source_target_pairs={{0,1},{1,0},{2,3},{3,2},{4,5},{5,4},{6,7},{7,6},{8,9},{9,8},{10,11... | collective-permute-start | bytes 1769480 | tf_op jit(solution)/shard_map/ppermute | solution.py:86
  341.4 15.9 %collective-permute-start.26 = (f32[16,288]{1,0:T(8,128)S(1)}, f32[16,288]{1,0:T(8,128)S(1)}, u32[]{:S(2)}, u32[]{:S(2)}) collective-permute-start(f32[16,288]{1,0:T(8,128)S(1)} %broadcast_select_fusion.16), channel_id=1, source_target_pairs={{0,16},{2,18},{4,20},{6,22},{8,24},{10,26},{12,28},{14,30},{16,0},... | collective-permute-start | bytes 55304 | tf_op jit(solution)/shard_map/ppermute | solution.py:82
  377.4 45.0 %collective-permute-start.56 = (bf16[16,96,768]{2,1,0:T(8,128)(2,1)}, bf16[16,96,768]{2,1,0:T(8,128)(2,1)S(1)}, u32[]{:S(2)}, u32[]{:S(2)}) collective-permute-start(bf16[16,96,768]{2,1,0:T(8,128)(2,1)} %get-tuple-element.102), channel_id=1, source_target_pairs={{0,1},{1,0},{2,3},{3,2},{4,5},{5,4},{6,7},{7,6},{8,9},{9,8},{10,11... | collective-permute-start | bytes 7077896 | tf_op jit(solution)/shard_map/ppermute | solution.py:86
  379.6 23.7 %collective-permute-start.25 = (bf16[1,640,768]{2,1,0:T(8,128)(2,1)}, bf16[1,640,768]{2,1,0:T(8,128)(2,1)S(1)}, u32[]{:S(2)}, u32[]{:S(2)}) collective-permute-start(bf16[1,640,768]{2,1,0:T(8,128)(2,1)} %broadcast_select_fusion.2), channel_id=1, source_target_pairs={{0,1},{1,0},{2,3},{3,2},{4,5},{5,4},{6,7},{7,6},{8,9},{9,8},{10,11... | collective-permute-start | bytes 2949128 | tf_op jit(solution)/shard_map/ppermute | solution.py:86
  381.1 26.4 %collective-permute-start.24 = (bf16[1,640,768]{2,1,0:T(8,128)(2,1)}, bf16[1,640,768]{2,1,0:T(8,128)(2,1)S(1)}, u32[]{:S(2)}, u32[]{:S(2)}) collective-permute-start(bf16[1,640,768]{2,1,0:T(8,128)(2,1)} %broadcast_select_fusion.6), channel_id=1, source_target_pairs={{0,1},{1,0},{2,3},{3,2},{4,5},{5,4},{6,7},{7,6},{8,9},{9,8},{10,11... | collective-permute-start | bytes 2949128 | tf_op jit(solution)/shard_map/ppermute | solution.py:86
  400.9 23.6 %collective-permute-start.51 = (bf16[16,24,3072]{2,1,0:T(8,128)(2,1)S(1)}, bf16[16,24,3072]{2,1,0:T(8,128)(2,1)S(1)}, u32[]{:S(2)}, u32[]{:S(2)}) collective-permute-start(bf16[16,24,3072]{2,1,0:T(8,128)(2,1)S(1)} %copy-done.15), channel_id=1, source_target_pairs={{0,1},{1,0},{2,3},{3,2},{4,5},{5,4},{6,7},{7,6},{8,9},{9,8},{10,11... | collective-permute-start | bytes 7077896 | tf_op jit(solution)/shard_map/ppermute | solution.py:86
  419.3 48.3 %collective-permute-start.50 = (bf16[1,24,768]{2,1,0:T(8,128)(2,1)S(1)}, bf16[1,24,768]{2,1,0:T(8,128)(2,1)S(1)}, u32[]{:S(2)}, u32[]{:S(2)}) collective-permute-start(bf16[1,24,768]{2,1,0:T(8,128)(2,1)S(1)} %add_convert_fusion.40), channel_id=1, source_target_pairs={{0,16},{2,18},{4,20},{6,22},{8,24},{10,26},{12,28},{14,30},{16,0},... | collective-permute-start | bytes 110600 | tf_op jit(solution)/shard_map/ppermute | solution.py:82
  424.4 24.2 %collective-permute-start.57 = (bf16[8,96,768]{2,1,0:T(8,128)(2,1)S(1)}, bf16[8,96,768]{2,1,0:T(8,128)(2,1)S(1)}, u32[]{:S(2)}, u32[]{:S(2)}) collective-permute-start(bf16[8,96,768]{2,1,0:T(8,128)(2,1)S(1)} %get-tuple-element.138), channel_id=1, source_target_pairs={{0,2},{2,0},{4,6},{6,4},{8,10},{10,8},{12,14},{14,12},{16,18},{18,... | collective-permute-start | bytes 3538952 | tf_op jit(solution)/shard_map/ppermute | solution.py:82
  426.4 27.9 %collective-permute-start.52 = (bf16[8,24,3072]{2,1,0:T(8,128)(2,1)S(1)}, bf16[8,24,3072]{2,1,0:T(8,128)(2,1)S(1)}, u32[]{:S(2)}, u32[]{:S(2)}) collective-permute-start(bf16[8,24,3072]{2,1,0:T(8,128)(2,1)S(1)} %get-tuple-element.140), channel_id=1, source_target_pairs={{0,4},{2,6},{4,0},{6,2},{8,12},{10,14},{12,8},{14,10},{16,20},{18,... | collective-permute-start | bytes 3538952 | tf_op jit(solution)/shard_map/ppermute | solution.py:82
  (56 other events, 424.0 us)
